TPU v7x, 32 devices: a whole 2x2x4 slice. The times are simulated.
32 devices in a mesh: groups: 2 (over x), dp: 16 (over z, y, core).
Axes of the slice: x: 2, y: 2, z: 4, core: 2. Of those that a mesh axis runs over, the one named last changes fastest.
Arguments:
- hidden_rows: bfloat16 [512, 16, 14336], P(('groups', 'dp')), parts along dimension 0
- output_grads: bfloat16 [512, 16, 4096], P(('groups', 'dp')), parts along dimension 0
- proj_in: bfloat16 [32, 14336], replicated, may hold values from -0.046875 to 0.046875
- proj_out: bfloat16 [32, 4096], replicated, may hold values from -0.09375 to 0.09375
- token_counts: int32 [512], P(('groups', 'dp')), parts along dimension 0, may hold values from 1 to 16
- query_vectors: float32 [256, 1024], P(('groups', 'dp')), parts along dimension 0, may hold values from -6 to 6
- query_slot: int32 [256], P('groups'), parts along dimension 0, may hold values from 0 to 127, each once
Outputs:
- scores: float32 [512, 128], P(('groups', 'dp')), parts along dimension 0
There are 2 independent parts, one for each index of `groups`. A program takes and returns all parts, laid end to end along the dimension named above; an argument that names none is the same for every part. Nothing has to cross between parts.
Inputs may be any that keep to these rules, and one draw needn't show every extreme that they name: `query_slot`: each of 0 to 127 once.
All inputs are finite; a program needn't handle non-finite values.
Results may differ from a plain program's by a relative error of at most 0.0003.
Values sent between devices are 32-bit elements; how exact they have to be, the bound alone decides.
No kernel may reach another device: no remote copies, remote signals or barrier semaphores. Data moves between devices by JAX's collectives and lax.ppermute only.
A program may use at most 128 MiB of HBM per device.

v0:
```python
import jax
import jax.numpy as jnp
from jax import lax
from jax.sharding import PartitionSpec as P

damp_share = 0.1


def shards(hidden_rows, output_grads, proj_in, proj_out, token_counts, query_vectors, query_slot):
    examples, seq, width = hidden_rows.shape
    rank = proj_in.shape[0]
    flat = rank * rank
    total = examples * lax.axis_size("dp")
    left = jnp.einsum("esf,rf->esr", hidden_rows, proj_in, preferred_element_type=jnp.float32)
    right = jnp.einsum("esd,rd->esr", output_grads, proj_out, preferred_element_type=jnp.float32)
    slots = jnp.arange(seq, dtype=jnp.int32)
    masking = (slots[None, :] < token_counts[:, None]).astype(jnp.float32)
    left = left * masking[:, :, None]
    outer = jnp.einsum("esr,esq->erq", left, right, precision=lax.Precision.HIGHEST)
    vectors = (outer / token_counts.astype(jnp.float32)[:, None, None]).reshape(examples, flat)
    partial_fisher = jnp.dot(vectors.T, vectors, precision=lax.Precision.HIGHEST)
    fisher = lax.psum(partial_fisher, "dp")
    fisher = fisher / jnp.float32(total)
    trace_value = lax.psum(jnp.sum(vectors * vectors), "dp") / jnp.float32(total)
    damped = fisher + damp_share * trace_value / flat * jnp.eye(flat, dtype=jnp.float32)
    chol = jnp.linalg.cholesky(damped)
    first = lax.linalg.triangular_solve(
        chol, query_vectors, left_side=False, lower=True, transpose_a=True
    )
    solved = lax.all_gather(
        lax.linalg.triangular_solve(chol, first, left_side=False, lower=True, transpose_a=False),
        "dp",
        axis=0,
        tiled=True,
    )
    ordered = solved[query_slot]
    return jnp.dot(vectors, ordered.T, precision=lax.Precision.HIGHEST)


def solution(mesh):
    return jax.shard_map(
        shards,
        mesh=mesh,
        in_specs=(
            P(("groups", "dp"), None, None),
            P(("groups", "dp"), None, None),
            P(),
            P(),
            P(("groups", "dp")),
            P(("groups", "dp"), None),
            P("groups"),
        ),
        out_specs=P(("groups", "dp"), None),
        check_vma=False,
    )
```

profile of v0, /device:TPU:0, one launch (start us, length us, event | category | flops | bytes accessed | tf_op | source)
XLA Modules:
  0.0 524.6 jit_solution(17998003281435064928)
XLA Ops:
  9.8 5.3 %convolution_multiply_fusion = f32[16,16,32]{2,1,0:T(8,128)S(1)} fusion(bf16[16,16,14336]{2,1,0:T(8,128)(2,1)} %param.7, bf16[32,14336]{1,0:T(8,128)(2,1)} %param.9, f32[16,16]{1,0:T(8,128)S(1)} %fusion.90), kind=kOutput, calls=%fused_computation.21 | convolution fusion | flops 234889216 | bytes 8291328 | tf_op jit(solution)/shard_map/esf,rf->esr/dot_general | solution.py:14
  16.6 5.0 fusion.99
  21.6 36.6 %psum.15 = f32[]{:T(128)} all-reduce(f32[]{:T(128)} %get-tuple-element.58), channel_id=1, replica_groups=mesh['groups'=2,'dp'=16] {'dp'}, use_global_device_ids=true, to_apply=%region_2.0 | all-reduce | flops 1 | bytes 8 | tf_op jit(solution)/shard_map/psum | solution.py:24
  58.8 77.2 %all-reduce.3.cloned.1.call-done = f32[1024,1024]{0,1:T(8,128)} async-done(((f32[1024,1024]{0,1:T(8,128)}), f32[1024,1024]{0,1:T(8,128)}) %all-reduce.3.cloned.1.call-update) | async-done | bytes 4194320 | tf_op jit(solution)/shard_map/psum | solution.py:22
  136.0 5.0 select_add_fusion
  141.1 5.5 %copy.9 = f32[1024,1024]{1,0:T(8,128)} copy(f32[1024,1024]{0,1:T(8,128)} %select_add_fusion) | data formatting | bytes 8388608 | tf_op jit(solution)/shard_map/add | solution.py:25
  146.6 4.5 fusion
  153.0 11.7 %cholesky.223 = f32[128,128]{1,0:T(8,128)S(1)} custom-call(f32[128,128]{1,0:T(8,128)S(1)} %cholesky.580), custom_call_target="Cholesky" | custom-call | tf_op jit(solution)/shard_map/jit(cholesky)/cholesky | solution.py:26
  165.4 9.8 %custom-call.64 = f32[1,128,128]{1,2,0:T(8,128)S(1)} custom-call(f32[1,128,128]{2,1,0:T(8,128)S(1)} %get-tuple-element.40), custom_call_target="InvertDiagBlocksLowerTriangular" | custom-call | tf_op jit(solution)/shard_map/jit(cholesky)/cholesky | solution.py:26
  178.6 11.7 %cholesky.244 = f32[128,128]{1,0:T(8,128)S(1)} custom-call(f32[128,128]{1,0:T(8,128)S(1)} %cholesky.584), custom_call_target="Cholesky" | custom-call | tf_op jit(solution)/shard_map/jit(cholesky)/cholesky | solution.py:26
  190.6 9.8 %custom-call.65 = f32[1,128,128]{1,2,0:T(8,128)S(1)} custom-call(f32[1,128,128]{2,1,0:T(8,128)S(1)} %get-tuple-element.38), custom_call_target="InvertDiagBlocksLowerTriangular" | custom-call | tf_op jit(solution)/shard_map/jit(cholesky)/cholesky | solution.py:26
  204.4 2.4 convolution_subtract_fusion.1
  206.8 11.7 %cholesky.468 = f32[128,128]{1,0:T(8,128)S(1)} custom-call(f32[128,128]{1,0:T(8,128)S(1)} %cholesky.589), custom_call_target="Cholesky" | custom-call | tf_op jit(solution)/shard_map/jit(cholesky)/cholesky | solution.py:26
  219.3 9.8 %custom-call.66 = f32[1,128,128]{1,2,0:T(8,128)S(1)} custom-call(f32[1,128,128]{2,1,0:T(8,128)S(1)} %get-tuple-element.36), custom_call_target="InvertDiagBlocksLowerTriangular" | custom-call | tf_op jit(solution)/shard_map/jit(cholesky)/cholesky | solution.py:26
  230.3 3.5 convolution_subtract_fusion.2
  233.9 11.7 %cholesky.487 = f32[128,128]{1,0:T(8,128)S(1)} custom-call(f32[128,128]{1,0:T(8,128)S(1)} %cholesky.594), custom_call_target="Cholesky" | custom-call | tf_op jit(solution)/shard_map/jit(cholesky)/cholesky | solution.py:26
  246.4 9.8 %custom-call.67 = f32[1,128,128]{1,2,0:T(8,128)S(1)} custom-call(f32[1,128,128]{2,1,0:T(8,128)S(1)} %get-tuple-element.34), custom_call_target="InvertDiagBlocksLowerTriangular" | custom-call | tf_op jit(solution)/shard_map/jit(cholesky)/cholesky | solution.py:26
  257.3 3.1 convolution_subtract_fusion.3
  260.5 11.9 %cholesky.506 = f32[128,128]{1,0:T(8,128)S(1)} custom-call(f32[128,128]{1,0:T(8,128)S(1)} %cholesky.599), custom_call_target="Cholesky" | custom-call | tf_op jit(solution)/shard_map/jit(cholesky)/cholesky | solution.py:26
  273.1 9.8 %custom-call.68 = f32[1,128,128]{1,2,0:T(8,128)S(1)} custom-call(f32[1,128,128]{2,1,0:T(8,128)S(1)} %get-tuple-element.32), custom_call_target="InvertDiagBlocksLowerTriangular" | custom-call | tf_op jit(solution)/shard_map/jit(cholesky)/cholesky | solution.py:26
  284.1 3.1 convolution_subtract_fusion.4
  287.2 11.7 %cholesky.526 = f32[128,128]{1,0:T(8,128)S(1)} custom-call(f32[128,128]{1,0:T(8,128)S(1)} %cholesky.604), custom_call_target="Cholesky" | custom-call | tf_op jit(solution)/shard_map/jit(cholesky)/cholesky | solution.py:26
  299.6 9.8 %custom-call.69 = f32[1,128,128]{1,2,0:T(8,128)S(1)} custom-call(f32[1,128,128]{2,1,0:T(8,128)S(1)} %get-tuple-element.30), custom_call_target="InvertDiagBlocksLowerTriangular" | custom-call | tf_op jit(solution)/shard_map/jit(cholesky)/cholesky | solution.py:26
  310.4 2.9 convolution_subtract_fusion.5
  313.3 11.7 %cholesky.546 = f32[128,128]{1,0:T(8,128)S(1)} custom-call(f32[128,128]{1,0:T(8,128)S(1)} %cholesky.609), custom_call_target="Cholesky" | custom-call | tf_op jit(solution)/shard_map/jit(cholesky)/cholesky | solution.py:26
  325.8 9.8 %custom-call.70 = f32[1,128,128]{1,2,0:T(8,128)S(1)} custom-call(f32[1,128,128]{2,1,0:T(8,128)S(1)} %get-tuple-element.28), custom_call_target="InvertDiagBlocksLowerTriangular" | custom-call | tf_op jit(solution)/shard_map/jit(cholesky)/cholesky | solution.py:26
  338.7 11.7 %cholesky.564 = f32[128,128]{1,0:T(8,128)S(1)} custom-call(f32[128,128]{1,0:T(8,128)S(1)} %convolution_subtract_fusion.6), custom_call_target="Cholesky" | custom-call | tf_op jit(solution)/shard_map/jit(cholesky)/cholesky | solution.py:26
  360.9 4.8 select_select_fusion
  365.7 28.5 %while.1 = (s32[]{:T(128)}, f32[1024,1024]{0,1:T(8,128)}, s32[8,2]{0,1:T(2,128)S(1)}, f32[8,128,128]{2,1,0:T(8,128)}, s32[]{:T(128)}) while((s32[]{:T(128)}, f32[1024,1024]{0,1:T(8,128)}, s32[8,2]{0,1:T(2,128)S(1)}, f32[8,128,128]{2,1,0:T(8,128)}, s32[]{:T(128)}) %tuple.50), condition=%wide.while_cond, body=%wide.while_body.sunk | while | flops 2 | bytes 393329 | solution.py:27
  369.9 2.2 dynamic-slice.7
  394.2 79.6 %custom-call.71 = f32[8,128,128]{1,2,0:T(8,128)S(1)} custom-call(f32[8,128,128]{2,1,0:T(8,128)} %get-tuple-element.12), custom_call_target="InvertDiagBlocksLowerTriangular" | custom-call | tf_op jit(solution)/shard_map/triangular_solve | solution.py:27
  494.6 20.8 %all_gather.3 = f32[128,1024]{1,0:T(8,128)S(1)} all-gather(f32[8,1024]{1,0:T(8,128)S(1)} %constant_dynamic-update-slice_fusion.36), channel_id=1, replica_groups=mesh['groups'=2,'dp'=16] {'dp'}, dimensions={0}, use_global_device_ids=true | all-gather | bytes 557056 | tf_op jit(solution)/shard_map/all_gather | solution.py:30
  (164 shorter events, 80.4 us)
Async XLA Ops:
  6.5 1.6 copy-start
  6.5 129.5 %all-reduce.3.cloned.1.call-start = ((), (), s32[]{:S(2)}) async-start(), calls=%async_computation | async-start | bytes 8388608 | tf_op jit(solution)/shard_map/psum | solution.py:22
  16.5 42.3 %copy-start.4 = (s32[128]{0:T(128)S(1)}, s32[128]{0:T(128)}, u32[]{:S(2)}) copy-start(s32[128]{0:T(128)} %param.13) | copy-start | bytes 1540
  151.0 1.9 copy-start.2
  202.4 2.0 copy-start.1
  360.9 113.0 %copy-start.3 = (f32[8,1024]{1,0:T(8,128)S(1)}, f32[8,1024]{1,0:T(8,128)}, u32[]{:S(2)}) copy-start(f32[8,1024]{1,0:T(8,128)} %param.12) | copy-start | bytes 98308
Sparse Core Ops, SparseCore 0:
  21.7 114.2 all-reduce.2
where the time goes:
time: 531 us; the launch traced here: 525 us
  other arithmetic  263 us (50%)
  waiting for transfers between devices  77.2 us (15%)
  matrix products  60.9 us (11%)
  blocking collectives  57.4 us (11%)
  local copies, waits for them, and re-layouts  46.1 us (9%)
  between operations  20 us (4%)
    another operation x30, other arithmetic, shards(): chol = jnp.linalg.cholesky(damped)  167 us
    another operation x3, other arithmetic, shards(): lax.linalg.triangular_solve(chol, query_vectors, left_side=False, lower=T...  84.5 us
    psum x1, waiting for transfers between devices, shards(): fisher = lax.psum(partial_fisher, 'dp')  77.2 us
    psum x1, blocking collectives, shards(): lax.psum(jnp.sum(vectors * vectors), 'dp') / jnp.float32(total)  36.6 us
    another operation x40, local copies, waits for them, and re-layouts  28.4 us
    another operation x14, matrix products, shards(): chol = jnp.linalg.cholesky(damped)  26.1 us
    all_gather x1, blocking collectives, shards(): lax.all_gather(lax.linalg.triangular_solve(chol, first, left_side=False,...  20.8 us
    another operation x15, matrix products, shards(): lax.linalg.triangular_solve(chol, first, left_side=False, lower=True, tra...  10.7 us
  transfers between devices with their start and end apart: 1, of which 1 were waited for; matrix products, arithmetic and copies ran while one was open for 0% of the time, Pallas kernels for 0%

commit v1 on v0

v1 whole, which is shorter than its diff:
```python
import functools

import jax
import jax.numpy as jnp
from jax import lax
from jax.experimental import pallas as pl
from jax.experimental.pallas import tpu as pltpu
from jax.sharding import PartitionSpec as P

damp_share = 0.1
f32 = jnp.float32
bf16 = jnp.bfloat16
levels = 9
vmem_bytes = 60 * 2**20


def split3(x):
    high = x.astype(bf16)
    rest = x - high.astype(f32)
    mid = rest.astype(bf16)
    low = (rest - mid.astype(f32)).astype(bf16)
    return high, mid, low


def nt(a, b):
    return lax.dot_general(a, b, (((1,), (1,)), ((), ())), preferred_element_type=f32)


def nn(a, b):
    return jnp.dot(a, b, preferred_element_type=f32)


def project_kernel(
    cuts, hidden, grads, pin, pout, counts, queries, out, hbuf, gbuf, pibuf, pobuf, sems
):
    examples, seq, width = hbuf.shape
    model = gbuf.shape[2]
    rank = pibuf.shape[0]
    flat = rank * rank
    rows = examples * seq
    copies = [
        pltpu.make_async_copy(pout, pobuf, sems.at[0]),
        pltpu.make_async_copy(grads, gbuf, sems.at[1]),
        pltpu.make_async_copy(pin, pibuf, sems.at[2]),
    ]
    for i, (a, b) in enumerate(cuts):
        copies.append(
            pltpu.make_async_copy(
                hidden.at[:, :, a:b], hbuf.at[:, :, a:b], sems.at[3 + i]
            )
        )
    for copy in copies:
        copy.start()
    copies[0].wait()
    copies[1].wait()
    right = nt(gbuf[...].reshape(rows, model), pobuf[...])
    copies[2].wait()
    left = jnp.zeros((rows, rank), f32)
    for i, (a, b) in enumerate(cuts):
        copies[3 + i].wait()
        left = left + nt(hbuf[:, :, a:b].reshape(rows, b - a), pibuf[:, a:b])
    example = lax.broadcasted_iota(jnp.int32, (examples, 1), 0)
    live = jnp.zeros((examples, 1), jnp.int32)
    for e in range(examples):
        live = jnp.where(example == e, counts[e], live)
    to = lax.broadcasted_iota(jnp.int32, (seq, examples, rows), 1)
    slot = lax.broadcasted_iota(jnp.int32, (seq, examples, rows), 0)
    source = lax.broadcasted_iota(jnp.int32, (seq, examples, rows), 2)
    chosen = (source == to * seq + slot) & (slot < live[None])
    pick = jnp.where(chosen, 1.0, 0.0).astype(bf16).reshape(rows, rows)
    parts = jnp.concatenate(split3(left) + split3(right), axis=1)
    parts = nn(pick, parts).astype(bf16)
    wide = 3 * rank
    column = lax.broadcasted_iota(jnp.int32, (wide, flat), 1)
    row = lax.broadcasted_iota(jnp.int32, (wide, flat), 0) % rank
    spread = jnp.where(row == column // rank, 1.0, 0.0).astype(bf16)
    tile = jnp.where(row == column % rank, 1.0, 0.0).astype(bf16)
    over = live.astype(f32)
    step = 256
    for c in range(0, flat, step):
        product = nn(parts[:, :wide], spread[:, c : c + step]) * nn(
            parts[:, wide:], tile[:, c : c + step]
        )
        total = jnp.sum(product.reshape(seq, examples, step), axis=0)
        out[:examples, c : c + step] = total / over
    out[examples:] = queries[...]


def project(hidden_rows, output_grads, proj_in, proj_out, token_counts, queries):
    examples, seq, width = hidden_rows.shape
    model = output_grads.shape[2]
    rank = proj_in.shape[0]
    pieces = 7 if width % (7 * 128) == 0 else 1
    size = width // pieces
    cuts = tuple((i * size, (i + 1) * size) for i in range(pieces))
    anywhere = pl.BlockSpec(memory_space=pl.ANY)
    return pl.pallas_call(
        functools.partial(project_kernel, cuts),
        out_shape=jax.ShapeDtypeStruct((examples + queries.shape[0], rank * rank), f32),
        in_specs=[anywhere] * 4 + [
            pl.BlockSpec(memory_space=pltpu.SMEM),
            pl.BlockSpec(memory_space=pltpu.VMEM),
        ],
        out_specs=pl.BlockSpec(memory_space=pltpu.VMEM),
        scratch_shapes=[
            pltpu.VMEM(hidden_rows.shape, bf16),
            pltpu.VMEM(output_grads.shape, bf16),
            pltpu.VMEM(proj_in.shape, bf16),
            pltpu.VMEM(proj_out.shape, bf16),
            pltpu.SemaphoreType.DMA((3 + pieces,)),
        ],
        compiler_params=pltpu.CompilerParams(vmem_limit_bytes=vmem_bytes),
        name="project",
    )(hidden_rows, output_grads, proj_in, proj_out, token_counts, queries)


def square_parts(x, n, passes):
    high, mid, low = split3(x)
    if passes == 6:
        left = [high, high, mid, mid, high, low]
        right = [high, mid, high, mid, low, high]
    else:
        left = [high, high, mid]
        right = [high, mid, high]
    return nn(
        jnp.concatenate(left, axis=1),
        jnp.concatenate([r[:n] for r in right], axis=0),
    )


def solve_kernel(total, each, blocks, *refs):
    bs = refs[:blocks]
    slots, out, high, mid, low, held = refs[blocks:]
    tall, flat = bs[0].shape
    ask = tall - each
    n = each * blocks
    asked = ask * blocks
    squares = jnp.zeros((each, flat), f32)
    for i in range(blocks):
        v = bs[i][:each]
        squares = squares + v * v
        h, m, l = split3(v)
        high[i * each : (i + 1) * each] = h
        mid[i * each : (i + 1) * each] = m
        low[i * each : (i + 1) * each] = l
    h, m, l = split3(jnp.concatenate([b[each:] for b in bs], axis=0))
    high[n:] = h
    mid[n:] = m
    low[n:] = l
    trace = jnp.sum(squares, keepdims=True)
    hv, mv, lv = high[:n], mid[:n], low[:n]
    products = nt(high[...], hv) + (
        (nt(high[...], mv) + nt(mid[...], hv))
        + (nt(mid[...], mv) + nt(high[...], lv) + nt(low[...], hv))
    )
    gram = products[:n] / trace
    y = products[n:]
    scale = 2.0 * lax.rsqrt(jnp.sum(gram * gram, keepdims=True))
    d = gram * scale
    e = scale * (damp_share / flat)
    for level in range(levels - 1):
        both = jnp.concatenate([d, y], axis=0)
        w = square_parts(both, n, 6 if level < 4 else 3)
        d = 4.0 * d - 2.0 * w[:n]
        y = y - w[n:] * (1.0 / (e + 2.0))
        e = 2.0 * e * (e + 2.0)
    dh, dm, _ = split3(d)
    yh, ym, _ = split3(y)
    y = y - (nn(yh, dh) + (nn(yh, dm) + nn(ym, dh))) * (1.0 / (e + 2.0))
    e = 2.0 * e * (e + 2.0)
    held[...] = y
    short = e < 1e6
    last = jnp.where(short, 2.0 * e * (e + 2.0), e)

    @pl.when(e[0, 0] < 1e6)
    def _():
        w = square_parts(d, n, 3)
        more = 4.0 * d - 2.0 * w
        mh, mm, _ = split3(more)
        now = held[...]
        nh, nm, _ = split3(now)
        held[...] = now - (nn(nh, mh) + (nn(nh, mm) + nn(nm, mh))) * (1.0 / (e + 2.0))

    factor = (flat * total / damp_share) / trace * (last / (1.0 + last))
    mine = held[:, :each] * factor
    place = lax.broadcasted_iota(jnp.int32, (asked, asked), 0) ^ (ask * lax.axis_index("dp"))
    pick = jnp.where(place == slots[...], 1.0, 0.0).astype(bf16)
    a, b, c = split3(mine)
    tn = (((0,), (0,)), ((), ()))
    out[...] = (
        lax.dot_general(a, pick, tn, preferred_element_type=f32)
        + lax.dot_general(b, pick, tn, preferred_element_type=f32)
        + lax.dot_general(c, pick, tn, preferred_element_type=f32)
    )


def solve(total, each, blocks, slots):
    tall, flat = blocks[0].shape
    asked = slots.shape[0]
    n = each * len(blocks)
    return pl.pallas_call(
        functools.partial(solve_kernel, total, each, len(blocks)),
        out_shape=jax.ShapeDtypeStruct((each, asked), f32),
        in_specs=[pl.BlockSpec(memory_space=pltpu.VMEM)] * (len(blocks) + 1),
        out_specs=pl.BlockSpec(memory_space=pltpu.VMEM),
        scratch_shapes=[
            pltpu.VMEM((n + asked, flat), bf16),
            pltpu.VMEM((n + asked, flat), bf16),
            pltpu.VMEM((n + asked, flat), bf16),
            pltpu.VMEM((asked, n), f32),
        ],
        compiler_params=pltpu.CompilerParams(vmem_limit_bytes=vmem_bytes),
        name="solve",
    )(*blocks, slots.reshape(1, asked))


def flip(x, bits, size):
    return lax.ppermute(x, "dp", [(i, i ^ bits) for i in range(size)])


def gather_blocks(rows, size):
    got = {0: rows, 8: flip(rows, 8, size)}
    for k in (2, 4, 6):
        got[k] = flip(rows, k, size)
    for k in (2, 4, 6):
        got[8 + k] = flip(got[8], k, size)
    for k in range(0, size, 2):
        got[k + 1] = flip(got[k], 1, size)
    return [got[k] for k in range(size)]


def dual(hidden_rows, output_grads, proj_in, proj_out, token_counts, query_vectors, query_slot):
    size = lax.axis_size("dp")
    total = hidden_rows.shape[0] * size
    rows = project(hidden_rows, output_grads, proj_in, proj_out, token_counts, query_vectors)
    blocks = gather_blocks(rows, size)
    return solve(total, hidden_rows.shape[0], blocks, query_slot)


def primal(hidden_rows, output_grads, proj_in, proj_out, token_counts, query_vectors, query_slot):
    examples, seq, width = hidden_rows.shape
    rank = proj_in.shape[0]
    flat = rank * rank
    total = examples * lax.axis_size("dp")
    left = jnp.einsum("esf,rf->esr", hidden_rows, proj_in, preferred_element_type=f32)
    right = jnp.einsum("esd,rd->esr", output_grads, proj_out, preferred_element_type=f32)
    slots = jnp.arange(seq, dtype=jnp.int32)
    masking = (slots[None, :] < token_counts[:, None]).astype(f32)
    left = left * masking[:, :, None]
    outer = jnp.einsum("esr,esq->erq", left, right, precision=lax.Precision.HIGHEST)
    vectors = (outer / token_counts.astype(f32)[:, None, None]).reshape(examples, flat)
    partial_fisher = jnp.dot(vectors.T, vectors, precision=lax.Precision.HIGHEST)
    fisher = lax.psum(partial_fisher, "dp")
    fisher = fisher / f32(total)
    trace_value = lax.psum(jnp.sum(vectors * vectors), "dp") / f32(total)
    damped = fisher + damp_share * trace_value / flat * jnp.eye(flat, dtype=f32)
    chol = jnp.linalg.cholesky(damped)
    first = lax.linalg.triangular_solve(
        chol, query_vectors, left_side=False, lower=True, transpose_a=True
    )
    solved = lax.all_gather(
        lax.linalg.triangular_solve(chol, first, left_side=False, lower=True, transpose_a=False),
        "dp",
        axis=0,
        tiled=True,
    )
    ordered = solved[query_slot]
    return jnp.dot(vectors, ordered.T, precision=lax.Precision.HIGHEST)


def shards(hidden_rows, *rest):
    size = lax.axis_size("dp")
    examples, seq, _ = hidden_rows.shape
    asked = rest[4].shape[0]
    if size == 16 and examples == 16 and seq == 16 and asked == 8:
        return dual(hidden_rows, *rest)
    return primal(hidden_rows, *rest)


def solution(mesh):
    return jax.shard_map(
        shards,
        mesh=mesh,
        in_specs=(
            P(("groups", "dp"), None, None),
            P(("groups", "dp"), None, None),
            P(),
            P(),
            P(("groups", "dp")),
            P(("groups", "dp"), None),
            P("groups"),
        ),
        out_specs=P(("groups", "dp"), None),
        check_vma=False,
    )
```

time: 531 us -> 39.7 us (0.07); the launches traced: 525 us -> 39.8 us
  other arithmetic: 263 us -> 0 us
  waiting for transfers between devices: 77.2 us -> 7.13 us
  matrix products: 60.9 us -> 0 us
  blocking collectives: 57.4 us -> 0 us
  local copies, waits for them, and re-layouts: 46.1 us -> 0.57 us
  between operations: 20 us -> 0.15 us
  Pallas kernels: 0 us -> 19.4 us
  starting transfers between devices: 0.01 us -> 12.5 us
    another operation x33 -> x0, other arithmetic: 252 us -> none  [the longest x30 167 us: shards(): chol = jnp.linalg.cholesky(damped)]
    psum x1 -> x0, waiting for transfers between devices: 77.2 us -> none  [shards(): fisher = lax.psum(partial_fisher, 'dp')]
    another operation x44 -> x0, matrix products: 46.5 us -> none  [the longest x14 26.1 us: shards(): chol = jnp.linalg.cholesky(damped)]
    psum x1 -> x0, blocking collectives: 36.6 us -> none  [shards(): lax.psum(jnp.sum(vectors * vectors), 'dp') / jnp.float32(total)]
    another operation x70 -> x0, local copies, waits for them, and re-layouts: 35.5 us -> none
    all_gather x1 -> x0, blocking collectives: 20.8 us -> none  [shards(): lax.all_gather(lax.linalg.triangular_solve(chol, first, left_side=False,...]
    pallas_call x0 -> x2, Pallas kernels: none -> 19.4 us  [the longest x1 10.1 us: solve(): pl.pallas_call(functools.partial(solve_kernel, total, each, len(blocks)),...]
    dot_general x5 -> x0, matrix products: 14.4 us -> none  [the longest x1 5.34 us: shards(): jnp.einsum('esf,rf->esr', hidden_rows, proj_in, preferred_element_type=jn...]
  transfers between devices with their start and end apart: 1 -> 15, of which waited for: 1 -> 9; matrix products, arithmetic and copies ran while one was open for 0% -> 0% of each run, Pallas kernels for 0% -> 0%
where the time goes in v1:
time: 39.7 us; the launch traced here: 39.8 us
  Pallas kernels  19.4 us (49%)
  starting transfers between devices  12.5 us (31%)
  waiting for transfers between devices  7.13 us (18%)
  local copies, waits for them, and re-layouts  0.57 us (1%)
    ppermute x15, starting transfers between devices, flip(): return lax.ppermute(x, 'dp', [(i, i ^ bits) for i in range(size)])  12.5 us
    pallas_call x1, Pallas kernels, solve(): pl.pallas_call(functools.partial(solve_kernel, total, each, len(blocks)),...  10.1 us
    pallas_call x1, Pallas kernels, project(): pl.pallas_call(functools.partial(project_kernel, cuts), out_shape=jax.Sha...  9.33 us
    ppermute x15, waiting for transfers between devices, flip(): return lax.ppermute(x, 'dp', [(i, i ^ bits) for i in range(size)])  7.13 us
  transfers between devices with their start and end apart: 15, of which 9 were waited for; matrix products, arithmetic and copies ran while one was open for 0% of the time, Pallas kernels for 0%

profile of v1, /device:TPU:0, one launch (start us, length us, event | category | flops | bytes accessed | tf_op | source)
XLA Modules:
  0.0 39.8 jit_solution(7984802213845645130)
XLA Ops:
  0.0 9.3 %project.1.refs_0_ = f32[24,1024]{1,0:T(8,128)} custom-call(bf16[16,16,14336]{2,1,0:T(8,128)(2,1)} %hidden.1, bf16[16,16,4096]{2,1,0:T(8,128)(2,1)} %grads.1, bf16[32,14336]{1,0:T(8,128)(2,1)} %pin.1, bf16[32,4096]{1,0:T(8,128)(2,1)} %pout.1, s32[16]{0:T(128)} %counts.1, f32[8,1024]{1,0:T(8,128)} %queries.1), custom_call_target="tpu_custom_call" | custom-call | tf_op jit(solution)/shard_map/project/pallas_call | solution.py:97
  9.3 4.1 %collective-permute-start.7 = (f32[24,1024]{1,0:T(8,128)}, f32[24,1024]{1,0:T(8,128)S(1)}, u32[]{:S(2)}, u32[]{:S(2)}) collective-permute-start(f32[24,1024]{1,0:T(8,128)} %project.1.refs_0_), channel_id=1, source_target_pairs={{0,8},{1,9},{2,10},{3,11},{4,12},{5,13},{6,14},{7,15},{8,0},{9,1},... | collective-permute-start | bytes 294920 | tf_op jit(solution)/shard_map/ppermute | solution.py:218
  13.4 2.5 %collective-permute-start.5 = (f32[24,1024]{1,0:T(8,128)}, f32[24,1024]{1,0:T(8,128)S(1)}, u32[]{:S(2)}, u32[]{:S(2)}) collective-permute-start(f32[24,1024]{1,0:T(8,128)} %project.1.refs_0_), channel_id=1, source_target_pairs={{0,6},{1,7},{2,4},{3,5},{4,2},{5,3},{6,0},{7,1},{8,14},{9,15},{10,... | collective-permute-start | bytes 294920 | tf_op jit(solution)/shard_map/ppermute | solution.py:218
  16.0 0.4 %collective-permute-start.3 = (f32[24,1024]{1,0:T(8,128)}, f32[24,1024]{1,0:T(8,128)S(1)}, u32[]{:S(2)}, u32[]{:S(2)}) collective-permute-start(f32[24,1024]{1,0:T(8,128)} %project.1.refs_0_), channel_id=1, source_target_pairs={{0,4},{1,5},{2,6},{3,7},{4,0},{5,1},{6,2},{7,3},{8,12},{9,13},{10,... | collective-permute-start | bytes 294920 | tf_op jit(solution)/shard_map/ppermute | solution.py:218
  16.4 0.5 %collective-permute-start.1 = (f32[24,1024]{1,0:T(8,128)}, f32[24,1024]{1,0:T(8,128)S(1)}, u32[]{:S(2)}, u32[]{:S(2)}) collective-permute-start(f32[24,1024]{1,0:T(8,128)} %project.1.refs_0_), channel_id=1, source_target_pairs={{0,2},{1,3},{2,0},{3,1},{4,6},{5,7},{6,4},{7,5},{8,10},{9,11},{10,... | collective-permute-start | bytes 294920 | tf_op jit(solution)/shard_map/ppermute | solution.py:218
  16.9 0.0 collective-permute-start
  16.9 1.5 %collective-permute-done.7.refs_8_ = f32[24,1024]{1,0:T(8,128)S(1)} collective-permute-done((f32[24,1024]{1,0:T(8,128)}, f32[24,1024]{1,0:T(8,128)S(1)}, u32[]{:S(2)}, u32[]{:S(2)}) %collective-permute-start.7) | collective-permute-done | bytes 98336 | tf_op jit(solution)/shard_map/ppermute | solution.py:218
  18.5 1.9 %collective-permute-start.13 = (f32[24,1024]{1,0:T(8,128)S(1)}, f32[24,1024]{1,0:T(8,128)S(1)}, u32[]{:S(2)}, u32[]{:S(2)}) collective-permute-start(f32[24,1024]{1,0:T(8,128)S(1)} %collective-permute-done.7.refs_8_), channel_id=1, source_target_pairs={{0,6},{1,7},{2,4},{3,5},{4,2},{5,3},{6,0},{7,1},{8,14},{9,15},{10,... | collective-permute-start | bytes 294920 | tf_op jit(solution)/shard_map/ppermute | solution.py:218
  20.4 0.6 %collective-permute-done.5.refs_6_ = f32[24,1024]{1,0:T(8,128)S(1)} collective-permute-done((f32[24,1024]{1,0:T(8,128)}, f32[24,1024]{1,0:T(8,128)S(1)}, u32[]{:S(2)}, u32[]{:S(2)}) %collective-permute-start.5) | collective-permute-done | bytes 98336 | tf_op jit(solution)/shard_map/ppermute | solution.py:218
  21.0 1.3 %collective-permute-start.11 = (f32[24,1024]{1,0:T(8,128)S(1)}, f32[24,1024]{1,0:T(8,128)S(1)}, u32[]{:S(2)}, u32[]{:S(2)}) collective-permute-start(f32[24,1024]{1,0:T(8,128)S(1)} %collective-permute-done.7.refs_8_), channel_id=1, source_target_pairs={{0,4},{1,5},{2,6},{3,7},{4,0},{5,1},{6,2},{7,3},{8,12},{9,13},{10,... | collective-permute-start | bytes 294920 | tf_op jit(solution)/shard_map/ppermute | solution.py:218
  22.3 0.3 collective-permute-done.3.refs_4_
  22.6 0.6 %collective-permute-start.9 = (f32[24,1024]{1,0:T(8,128)S(1)}, f32[24,1024]{1,0:T(8,128)S(1)}, u32[]{:S(2)}, u32[]{:S(2)}) collective-permute-start(f32[24,1024]{1,0:T(8,128)S(1)} %collective-permute-done.7.refs_8_), channel_id=1, source_target_pairs={{0,2},{1,3},{2,0},{3,1},{4,6},{5,7},{6,4},{7,5},{8,10},{9,11},{10,... | collective-permute-start | bytes 294920 | tf_op jit(solution)/shard_map/ppermute | solution.py:218
  23.2 0.0 collective-permute-start.8
  23.2 0.0 collective-permute-done.refs_1_
  23.2 0.5 %collective-permute-start.6 = (f32[24,1024]{1,0:T(8,128)S(1)}, f32[24,1024]{1,0:T(8,128)S(1)}, u32[]{:S(2)}, u32[]{:S(2)}) collective-permute-start(f32[24,1024]{1,0:T(8,128)S(1)} %collective-permute-done.5.refs_6_), channel_id=1, source_target_pairs={{0,1},{1,0},{2,3},{3,2},{4,5},{5,4},{6,7},{7,6},{8,9},{9,8},{10,11... | collective-permute-start | bytes 294920 | tf_op jit(solution)/shard_map/ppermute | solution.py:218
  23.7 1.4 %collective-permute-done.13.refs_14_ = f32[24,1024]{1,0:T(8,128)S(1)} collective-permute-done((f32[24,1024]{1,0:T(8,128)S(1)}, f32[24,1024]{1,0:T(8,128)S(1)}, u32[]{:S(2)}, u32[]{:S(2)}) %collective-permute-start.13) | collective-permute-done | bytes 98336 | tf_op jit(solution)/shard_map/ppermute | solution.py:218
  25.1 0.0 collective-permute-start.4
  25.1 0.9 %collective-permute-done.11.refs_12_ = f32[24,1024]{1,0:T(8,128)S(1)} collective-permute-done((f32[24,1024]{1,0:T(8,128)S(1)}, f32[24,1024]{1,0:T(8,128)S(1)}, u32[]{:S(2)}, u32[]{:S(2)}) %collective-permute-start.11) | collective-permute-done | bytes 98336 | tf_op jit(solution)/shard_map/ppermute | solution.py:218
  26.0 0.0 collective-permute-start.2
  26.0 1.2 %collective-permute-done.9.refs_10_ = f32[24,1024]{1,0:T(8,128)S(1)} collective-permute-done((f32[24,1024]{1,0:T(8,128)S(1)}, f32[24,1024]{1,0:T(8,128)S(1)}, u32[]{:S(2)}, u32[]{:S(2)}) %collective-permute-start.9) | collective-permute-done | bytes 98336 | tf_op jit(solution)/shard_map/ppermute | solution.py:218
  27.2 0.0 collective-permute-done.8.refs_9_
  27.2 0.5 %collective-permute-start.12 = (f32[24,1024]{1,0:T(8,128)S(1)}, f32[24,1024]{1,0:T(8,128)S(1)}, u32[]{:S(2)}, u32[]{:S(2)}) collective-permute-start(f32[24,1024]{1,0:T(8,128)S(1)} %collective-permute-done.11.refs_12_), channel_id=1, source_target_pairs={{0,1},{1,0},{2,3},{3,2},{4,5},{5,4},{6,7},{7,6},{8,9},{9,8},{10,11... | collective-permute-start | bytes 294920 | tf_op jit(solution)/shard_map/ppermute | solution.py:218
  27.7 0.1 collective-permute-start.10
  27.8 0.0 collective-permute-done.4.refs_5_
  27.8 0.0 collective-permute-done.2.refs_3_
  27.8 0.7 %collective-permute-done.14.refs_15_ = f32[24,1024]{1,0:T(8,128)S(1)} collective-permute-done((f32[24,1024]{1,0:T(8,128)S(1)}, f32[24,1024]{1,0:T(8,128)S(1)}, u32[]{:S(2)}, u32[]{:S(2)}) %collective-permute-start.14) | collective-permute-done | bytes 98336 | tf_op jit(solution)/shard_map/ppermute | solution.py:218
  28.5 0.2 collective-permute-done.12.refs_13_
  28.7 0.4 collective-permute-done.10.refs_11_
  29.1 0.0 copy-done.12
  29.1 0.2 copy-done.13
  29.3 0.4 copy-done.14
  29.7 10.1 %solve.1 = f32[16,128]{1,0:T(8,128)} custom-call(f32[24,1024]{1,0:T(8,128)} %project.1.refs_0_, f32[24,1024]{1,0:T(8,128)} %copy-done.4, f32[24,1024]{1,0:T(8,128)} %copy-done.3, f32[24,1024]{1,0:T(8,128)} %copy-done.11, f32[24,1024]{1,0:T(8,128)} %copy-done.2, f32[24,1024]{1,0:T(8,128)} %copy-done.10, f32[24,1024]{1,0:T(8,128)} %copy-done.1, ...), custom_call_target="tpu_custom_call" | custom-call | tf_op jit(solution)/shard_map/solve/pallas_call | solution.py:201
  (30 shorter events, 0.1 us)
Async XLA Ops:
  9.3 9.1 %collective-permute-start.7 = (f32[24,1024]{1,0:T(8,128)}, f32[24,1024]{1,0:T(8,128)S(1)}, u32[]{:S(2)}, u32[]{:S(2)}) collective-permute-start(f32[24,1024]{1,0:T(8,128)} %project.1.refs_0_), channel_id=1, source_target_pairs={{0,8},{1,9},{2,10},{3,11},{4,12},{5,13},{6,14},{7,15},{8,0},{9,1},... | collective-permute-start | bytes 294920 | tf_op jit(solution)/shard_map/ppermute | solution.py:218
  13.4 7.6 %collective-permute-start.5 = (f32[24,1024]{1,0:T(8,128)}, f32[24,1024]{1,0:T(8,128)S(1)}, u32[]{:S(2)}, u32[]{:S(2)}) collective-permute-start(f32[24,1024]{1,0:T(8,128)} %project.1.refs_0_), channel_id=1, source_target_pairs={{0,6},{1,7},{2,4},{3,5},{4,2},{5,3},{6,0},{7,1},{8,14},{9,15},{10,... | collective-permute-start | bytes 294920 | tf_op jit(solution)/shard_map/ppermute | solution.py:218
  16.0 6.6 %collective-permute-start.3 = (f32[24,1024]{1,0:T(8,128)}, f32[24,1024]{1,0:T(8,128)S(1)}, u32[]{:S(2)}, u32[]{:S(2)}) collective-permute-start(f32[24,1024]{1,0:T(8,128)} %project.1.refs_0_), channel_id=1, source_target_pairs={{0,4},{1,5},{2,6},{3,7},{4,0},{5,1},{6,2},{7,3},{8,12},{9,13},{10,... | collective-permute-start | bytes 294920 | tf_op jit(solution)/shard_map/ppermute | solution.py:218
  16.4 6.8 %collective-permute-start.1 = (f32[24,1024]{1,0:T(8,128)}, f32[24,1024]{1,0:T(8,128)S(1)}, u32[]{:S(2)}, u32[]{:S(2)}) collective-permute-start(f32[24,1024]{1,0:T(8,128)} %project.1.refs_0_), channel_id=1, source_target_pairs={{0,2},{1,3},{2,0},{3,1},{4,6},{5,7},{6,4},{7,5},{8,10},{9,11},{10,... | collective-permute-start | bytes 294920 | tf_op jit(solution)/shard_map/ppermute | solution.py:218
  16.9 6.3 %collective-permute-start = (f32[24,1024]{1,0:T(8,128)}, f32[24,1024]{1,0:T(8,128)S(1)}, u32[]{:S(2)}, u32[]{:S(2)}) collective-permute-start(f32[24,1024]{1,0:T(8,128)} %project.1.refs_0_), channel_id=1, source_target_pairs={{0,1},{1,0},{2,3},{3,2},{4,5},{5,4},{6,7},{7,6},{8,9},{9,8},{10,11... | collective-permute-start | bytes 294920 | tf_op jit(solution)/shard_map/ppermute | solution.py:218
  18.5 10.6 %copy-start = (f32[24,1024]{1,0:T(8,128)}, f32[24,1024]{1,0:T(8,128)S(1)}, u32[]{:S(2)}) copy-start(f32[24,1024]{1,0:T(8,128)S(1)} %collective-permute-done.7.refs_8_) | copy-start | bytes 294916
  18.5 6.6 %collective-permute-start.13 = (f32[24,1024]{1,0:T(8,128)S(1)}, f32[24,1024]{1,0:T(8,128)S(1)}, u32[]{:S(2)}, u32[]{:S(2)}) collective-permute-start(f32[24,1024]{1,0:T(8,128)S(1)} %collective-permute-done.7.refs_8_), channel_id=1, source_target_pairs={{0,6},{1,7},{2,4},{3,5},{4,2},{5,3},{6,0},{7,1},{8,14},{9,15},{10,... | collective-permute-start | bytes 294920 | tf_op jit(solution)/shard_map/ppermute | solution.py:218
  21.0 8.0 %copy-start.1 = (f32[24,1024]{1,0:T(8,128)}, f32[24,1024]{1,0:T(8,128)S(1)}, u32[]{:S(2)}) copy-start(f32[24,1024]{1,0:T(8,128)S(1)} %collective-permute-done.5.refs_6_) | copy-start | bytes 294916
  21.0 5.0 %collective-permute-start.11 = (f32[24,1024]{1,0:T(8,128)S(1)}, f32[24,1024]{1,0:T(8,128)S(1)}, u32[]{:S(2)}, u32[]{:S(2)}) collective-permute-start(f32[24,1024]{1,0:T(8,128)S(1)} %collective-permute-done.7.refs_8_), channel_id=1, source_target_pairs={{0,4},{1,5},{2,6},{3,7},{4,0},{5,1},{6,2},{7,3},{8,12},{9,13},{10,... | collective-permute-start | bytes 294920 | tf_op jit(solution)/shard_map/ppermute | solution.py:218
  22.6 6.5 %copy-start.2 = (f32[24,1024]{1,0:T(8,128)}, f32[24,1024]{1,0:T(8,128)S(1)}, u32[]{:S(2)}) copy-start(f32[24,1024]{1,0:T(8,128)S(1)} %collective-permute-done.3.refs_4_) | copy-start | bytes 294916
  22.6 4.6 %collective-permute-start.9 = (f32[24,1024]{1,0:T(8,128)S(1)}, f32[24,1024]{1,0:T(8,128)S(1)}, u32[]{:S(2)}, u32[]{:S(2)}) collective-permute-start(f32[24,1024]{1,0:T(8,128)S(1)} %collective-permute-done.7.refs_8_), channel_id=1, source_target_pairs={{0,2},{1,3},{2,0},{3,1},{4,6},{5,7},{6,4},{7,5},{8,10},{9,11},{10,... | collective-permute-start | bytes 294920 | tf_op jit(solution)/shard_map/ppermute | solution.py:218
  23.2 5.9 %copy-start.3 = (f32[24,1024]{1,0:T(8,128)}, f32[24,1024]{1,0:T(8,128)S(1)}, u32[]{:S(2)}) copy-start(f32[24,1024]{1,0:T(8,128)S(1)} %collective-permute-done.1.refs_2_) | copy-start | bytes 294916
  23.2 4.0 %collective-permute-start.8 = (f32[24,1024]{1,0:T(8,128)S(1)}, f32[24,1024]{1,0:T(8,128)S(1)}, u32[]{:S(2)}, u32[]{:S(2)}) collective-permute-start(f32[24,1024]{1,0:T(8,128)S(1)} %collective-permute-done.7.refs_8_), channel_id=1, source_target_pairs={{0,1},{1,0},{2,3},{3,2},{4,5},{5,4},{6,7},{7,6},{8,9},{9,8},{10,11... | collective-permute-start | bytes 294920 | tf_op jit(solution)/shard_map/ppermute | solution.py:218
  23.2 5.9 %copy-start.4 = (f32[24,1024]{1,0:T(8,128)}, f32[24,1024]{1,0:T(8,128)S(1)}, u32[]{:S(2)}) copy-start(f32[24,1024]{1,0:T(8,128)S(1)} %collective-permute-done.refs_1_) | copy-start | bytes 294916
  23.2 4.5 %collective-permute-start.6 = (f32[24,1024]{1,0:T(8,128)S(1)}, f32[24,1024]{1,0:T(8,128)S(1)}, u32[]{:S(2)}, u32[]{:S(2)}) collective-permute-start(f32[24,1024]{1,0:T(8,128)S(1)} %collective-permute-done.5.refs_6_), channel_id=1, source_target_pairs={{0,1},{1,0},{2,3},{3,2},{4,5},{5,4},{6,7},{7,6},{8,9},{9,8},{10,11... | collective-permute-start | bytes 294920 | tf_op jit(solution)/shard_map/ppermute | solution.py:218
  25.1 4.0 %copy-start.5 = (f32[24,1024]{1,0:T(8,128)}, f32[24,1024]{1,0:T(8,128)S(1)}, u32[]{:S(2)}) copy-start(f32[24,1024]{1,0:T(8,128)S(1)} %collective-permute-done.13.refs_14_) | copy-start | bytes 294916
  25.1 2.7 %collective-permute-start.4 = (f32[24,1024]{1,0:T(8,128)S(1)}, f32[24,1024]{1,0:T(8,128)S(1)}, u32[]{:S(2)}, u32[]{:S(2)}) collective-permute-start(f32[24,1024]{1,0:T(8,128)S(1)} %collective-permute-done.3.refs_4_), channel_id=1, source_target_pairs={{0,1},{1,0},{2,3},{3,2},{4,5},{5,4},{6,7},{7,6},{8,9},{9,8},{10,11... | collective-permute-start | bytes 294920 | tf_op jit(solution)/shard_map/ppermute | solution.py:218
  26.0 3.0 %copy-start.6 = (f32[24,1024]{1,0:T(8,128)}, f32[24,1024]{1,0:T(8,128)S(1)}, u32[]{:S(2)}) copy-start(f32[24,1024]{1,0:T(8,128)S(1)} %collective-permute-done.11.refs_12_) | copy-start | bytes 294916
  26.0 1.8 %collective-permute-start.2 = (f32[24,1024]{1,0:T(8,128)S(1)}, f32[24,1024]{1,0:T(8,128)S(1)}, u32[]{:S(2)}, u32[]{:S(2)}) collective-permute-start(f32[24,1024]{1,0:T(8,128)S(1)} %collective-permute-done.1.refs_2_), channel_id=1, source_target_pairs={{0,1},{1,0},{2,3},{3,2},{4,5},{5,4},{6,7},{7,6},{8,9},{9,8},{10,11... | collective-permute-start | bytes 294920 | tf_op jit(solution)/shard_map/ppermute | solution.py:218
  27.2 1.9 %copy-start.7 = (f32[24,1024]{1,0:T(8,128)}, f32[24,1024]{1,0:T(8,128)S(1)}, u32[]{:S(2)}) copy-start(f32[24,1024]{1,0:T(8,128)S(1)} %collective-permute-done.9.refs_10_) | copy-start | bytes 294916
  27.2 1.3 %collective-permute-start.14 = (f32[24,1024]{1,0:T(8,128)S(1)}, f32[24,1024]{1,0:T(8,128)S(1)}, u32[]{:S(2)}, u32[]{:S(2)}) collective-permute-start(f32[24,1024]{1,0:T(8,128)S(1)} %collective-permute-done.13.refs_14_), channel_id=1, source_target_pairs={{0,1},{1,0},{2,3},{3,2},{4,5},{5,4},{6,7},{7,6},{8,9},{9,8},{10,11... | collective-permute-start | bytes 294920 | tf_op jit(solution)/shard_map/ppermute | solution.py:218
  27.2 1.9 %copy-start.8 = (f32[24,1024]{1,0:T(8,128)}, f32[24,1024]{1,0:T(8,128)S(1)}, u32[]{:S(2)}) copy-start(f32[24,1024]{1,0:T(8,128)S(1)} %collective-permute-done.8.refs_9_) | copy-start | bytes 294916
  27.2 1.4 %collective-permute-start.12 = (f32[24,1024]{1,0:T(8,128)S(1)}, f32[24,1024]{1,0:T(8,128)S(1)}, u32[]{:S(2)}, u32[]{:S(2)}) collective-permute-start(f32[24,1024]{1,0:T(8,128)S(1)} %collective-permute-done.11.refs_12_), channel_id=1, source_target_pairs={{0,1},{1,0},{2,3},{3,2},{4,5},{5,4},{6,7},{7,6},{8,9},{9,8},{10,11... | collective-permute-start | bytes 294920 | tf_op jit(solution)/shard_map/ppermute | solution.py:218
  27.7 1.4 %copy-start.9 = (f32[24,1024]{1,0:T(8,128)}, f32[24,1024]{1,0:T(8,128)S(1)}, u32[]{:S(2)}) copy-start(f32[24,1024]{1,0:T(8,128)S(1)} %collective-permute-done.6.refs_7_) | copy-start | bytes 294916
  27.7 1.3 %collective-permute-start.10 = (f32[24,1024]{1,0:T(8,128)S(1)}, f32[24,1024]{1,0:T(8,128)S(1)}, u32[]{:S(2)}, u32[]{:S(2)}) collective-permute-start(f32[24,1024]{1,0:T(8,128)S(1)} %collective-permute-done.9.refs_10_), channel_id=1, source_target_pairs={{0,1},{1,0},{2,3},{3,2},{4,5},{5,4},{6,7},{7,6},{8,9},{9,8},{10,11... | collective-permute-start | bytes 294920 | tf_op jit(solution)/shard_map/ppermute | solution.py:218
  27.8 1.3 %copy-start.10 = (f32[24,1024]{1,0:T(8,128)}, f32[24,1024]{1,0:T(8,128)S(1)}, u32[]{:S(2)}) copy-start(f32[24,1024]{1,0:T(8,128)S(1)} %collective-permute-done.4.refs_5_) | copy-start | bytes 294916
  27.8 1.3 %copy-start.11 = (f32[24,1024]{1,0:T(8,128)}, f32[24,1024]{1,0:T(8,128)S(1)}, u32[]{:S(2)}) copy-start(f32[24,1024]{1,0:T(8,128)S(1)} %collective-permute-done.2.refs_3_) | copy-start | bytes 294916
  28.5 0.6 %copy-start.12 = (f32[24,1024]{1,0:T(8,128)}, f32[24,1024]{1,0:T(8,128)S(1)}, u32[]{:S(2)}) copy-start(f32[24,1024]{1,0:T(8,128)S(1)} %collective-permute-done.14.refs_15_) | copy-start | bytes 294916
  28.7 0.6 %copy-start.13 = (f32[24,1024]{1,0:T(8,128)}, f32[24,1024]{1,0:T(8,128)S(1)}, u32[]{:S(2)}) copy-start(f32[24,1024]{1,0:T(8,128)S(1)} %collective-permute-done.12.refs_13_) | copy-start | bytes 294916
  29.0 0.6 %copy-start.14 = (f32[24,1024]{1,0:T(8,128)}, f32[24,1024]{1,0:T(8,128)S(1)}, u32[]{:S(2)}) copy-start(f32[24,1024]{1,0:T(8,128)S(1)} %collective-permute-done.10.refs_11_) | copy-start | bytes 294916

commit v2 on v1

--- a/solution.py
+++ b/solution.py
@@ -31,34 +31,44 @@
 
 
 def project_kernel(
-    cuts, hidden, grads, pin, pout, counts, queries, out, hbuf, gbuf, pibuf, pobuf, sems
+    size, hidden, grads, pin, pout, counts, queries, out, hbuf, gbuf, pibuf, pobuf, left, sems
 ):
-    examples, seq, width = hbuf.shape
+    pieces, examples, seq, _ = hbuf.shape
     model = gbuf.shape[2]
-    rank = pibuf.shape[0]
+    rank = pobuf.shape[0]
     flat = rank * rank
     rows = examples * seq
-    copies = [
+    first = [
         pltpu.make_async_copy(pout, pobuf, sems.at[0]),
         pltpu.make_async_copy(grads, gbuf, sems.at[1]),
-        pltpu.make_async_copy(pin, pibuf, sems.at[2]),
     ]
-    for i, (a, b) in enumerate(cuts):
-        copies.append(
+
+    def piece(i):
+        across = pl.ds(pl.multiple_of(i * size, 128), size)
+        return (
+            pltpu.make_async_copy(pin.at[:, across], pibuf.at[i], sems.at[2 + i]),
             pltpu.make_async_copy(
-                hidden.at[:, :, a:b], hbuf.at[:, :, a:b], sems.at[3 + i]
-            )
+                hidden.at[:, :, across], hbuf.at[i], sems.at[2 + pieces + i]
+            ),
         )
-    for copy in copies:
+
+    for copy in first:
         copy.start()
-    copies[0].wait()
-    copies[1].wait()
+    for i in range(pieces):
+        for copy in piece(i):
+            copy.start()
+    for copy in first:
+        copy.wait()
+    left[...] = jnp.zeros((rows, rank), f32)
     right = nt(gbuf[...].reshape(rows, model), pobuf[...])
-    copies[2].wait()
-    left = jnp.zeros((rows, rank), f32)
-    for i, (a, b) in enumerate(cuts):
-        copies[3 + i].wait()
-        left = left + nt(hbuf[:, :, a:b].reshape(rows, b - a), pibuf[:, a:b])
+
+    def work(i, carry):
+        for copy in piece(i):
+            copy.wait()
+        left[...] += nt(hbuf[i].reshape(rows, size), pibuf[i])
+        return carry
+
+    lax.fori_loop(0, pieces, work, 0)
     example = lax.broadcasted_iota(jnp.int32, (examples, 1), 0)
     live = jnp.zeros((examples, 1), jnp.int32)
     for e in range(examples):
@@ -68,7 +78,7 @@
     source = lax.broadcasted_iota(jnp.int32, (seq, examples, rows), 2)
     chosen = (source == to * seq + slot) & (slot < live[None])
     pick = jnp.where(chosen, 1.0, 0.0).astype(bf16).reshape(rows, rows)
-    parts = jnp.concatenate(split3(left) + split3(right), axis=1)
+    parts = jnp.concatenate(split3(left[...]) + split3(right), axis=1)
     parts = nn(pick, parts).astype(bf16)
     wide = 3 * rank
     column = lax.broadcasted_iota(jnp.int32, (wide, flat), 1)
@@ -90,12 +100,11 @@
     examples, seq, width = hidden_rows.shape
     model = output_grads.shape[2]
     rank = proj_in.shape[0]
-    pieces = 7 if width % (7 * 128) == 0 else 1
+    pieces = 4 if width % (4 * 128) == 0 else 1
     size = width // pieces
-    cuts = tuple((i * size, (i + 1) * size) for i in range(pieces))
     anywhere = pl.BlockSpec(memory_space=pl.ANY)
     return pl.pallas_call(
-        functools.partial(project_kernel, cuts),
+        functools.partial(project_kernel, size),
         out_shape=jax.ShapeDtypeStruct((examples + queries.shape[0], rank * rank), f32),
         in_specs=[anywhere] * 4 + [
             pl.BlockSpec(memory_space=pltpu.SMEM),
@@ -103,86 +112,66 @@
         ],
         out_specs=pl.BlockSpec(memory_space=pltpu.VMEM),
         scratch_shapes=[
-            pltpu.VMEM(hidden_rows.shape, bf16),
+            pltpu.VMEM((pieces, examples, seq, size), bf16),
             pltpu.VMEM(output_grads.shape, bf16),
-            pltpu.VMEM(proj_in.shape, bf16),
+            pltpu.VMEM((pieces, rank, size), bf16),
             pltpu.VMEM(proj_out.shape, bf16),
-            pltpu.SemaphoreType.DMA((3 + pieces,)),
+            pltpu.VMEM((examples * seq, rank), f32),
+            pltpu.SemaphoreType.DMA((2 + 2 * pieces,)),
         ],
         compiler_params=pltpu.CompilerParams(vmem_limit_bytes=vmem_bytes),
         name="project",
     )(hidden_rows, output_grads, proj_in, proj_out, token_counts, queries)
 
 
-def square_parts(x, n, passes):
+def times(x, n, passes):
     high, mid, low = split3(x)
-    if passes == 6:
-        left = [high, high, mid, mid, high, low]
-        right = [high, mid, high, mid, low, high]
-    else:
-        left = [high, high, mid]
-        right = [high, mid, high]
-    return nn(
-        jnp.concatenate(left, axis=1),
-        jnp.concatenate([r[:n] for r in right], axis=0),
-    )
+    total = nt(high, high[:n]) + (nt(high, mid[:n]) + nt(mid, high[:n]))
+    if passes > 3:
+        total = total + nt(mid, mid[:n])
+    if passes > 4:
+        total = total + (nt(high, low[:n]) + nt(low, high[:n]))
+    return total
 
 
 def solve_kernel(total, each, blocks, *refs):
     bs = refs[:blocks]
-    slots, out, high, mid, low, held = refs[blocks:]
+    slots, out, held = refs[blocks:]
     tall, flat = bs[0].shape
     ask = tall - each
     n = each * blocks
     asked = ask * blocks
-    squares = jnp.zeros((each, flat), f32)
-    for i in range(blocks):
-        v = bs[i][:each]
-        squares = squares + v * v
-        h, m, l = split3(v)
-        high[i * each : (i + 1) * each] = h
-        mid[i * each : (i + 1) * each] = m
-        low[i * each : (i + 1) * each] = l
-    h, m, l = split3(jnp.concatenate([b[each:] for b in bs], axis=0))
-    high[n:] = h
-    mid[n:] = m
-    low[n:] = l
+
+    squares = jnp.zeros((1, n), f32)
+    for k in range(0, flat, n):
+        x = jnp.concatenate(
+            [b[:each, k : k + n] for b in bs] + [b[each:, k : k + n] for b in bs], axis=0
+        )
+        w = times(x, n, 6)
+        held[...] = w if k == 0 else held[...] + w
+        squares = squares + jnp.sum(x[:n] * x[:n], axis=0, keepdims=True)
     trace = jnp.sum(squares, keepdims=True)
-    hv, mv, lv = high[:n], mid[:n], low[:n]
-    products = nt(high[...], hv) + (
-        (nt(high[...], mv) + nt(mid[...], hv))
-        + (nt(mid[...], mv) + nt(high[...], lv) + nt(low[...], hv))
-    )
-    gram = products[:n] / trace
-    y = products[n:]
+    gram = held[:n] * (1.0 / trace)
     scale = 2.0 * lax.rsqrt(jnp.sum(gram * gram, keepdims=True))
-    d = gram * scale
+    held[:n] = gram * scale
     e = scale * (damp_share / flat)
-    for level in range(levels - 1):
-        both = jnp.concatenate([d, y], axis=0)
-        w = square_parts(both, n, 6 if level < 4 else 3)
-        d = 4.0 * d - 2.0 * w[:n]
-        y = y - w[n:] * (1.0 / (e + 2.0))
-        e = 2.0 * e * (e + 2.0)
-    dh, dm, _ = split3(d)
-    yh, ym, _ = split3(y)
-    y = y - (nn(yh, dh) + (nn(yh, dm) + nn(ym, dh))) * (1.0 / (e + 2.0))
-    e = 2.0 * e * (e + 2.0)
-    held[...] = y
-    short = e < 1e6
-    last = jnp.where(short, 2.0 * e * (e + 2.0), e)
-
-    @pl.when(e[0, 0] < 1e6)
-    def _():
-        w = square_parts(d, n, 3)
-        more = 4.0 * d - 2.0 * w
-        mh, mm, _ = split3(more)
-        now = held[...]
-        nh, nm, _ = split3(now)
-        held[...] = now - (nn(nh, mh) + (nn(nh, mm) + nn(nm, mh))) * (1.0 / (e + 2.0))
-
-    factor = (flat * total / damp_share) / trace * (last / (1.0 + last))
-    mine = held[:, :each] * factor
+    ahead = e
+    for _ in range(levels):
+        ahead = 2.0 * ahead * (ahead + 2.0)
+    short = ahead < 1e6
+
+    def double(passes, level, e):
+        x = held[...]
+        w = times(x, n, passes)
+        held[:n] = 4.0 * x[:n] - 2.0 * w[:n]
+        held[n:] = x[n:] - w[n:] * (1.0 / (e + 2.0))
+        return 2.0 * e * (e + 2.0)
+
+    e = lax.fori_loop(0, 4, functools.partial(double, 6), e)
+    more = jnp.where(jnp.sum(jnp.where(short, 1.0, 0.0)) > 0.5, 1, 0)
+    e = lax.fori_loop(4, levels + more, functools.partial(double, 3), e)
+    factor = (flat * total / damp_share) / trace * (e / (1.0 + e))
+    mine = held[n:, :each] * factor
     place = lax.broadcasted_iota(jnp.int32, (asked, asked), 0) ^ (ask * lax.axis_index("dp"))
     pick = jnp.where(place == slots[...], 1.0, 0.0).astype(bf16)
     a, b, c = split3(mine)
@@ -203,12 +192,7 @@
         out_shape=jax.ShapeDtypeStruct((each, asked), f32),
         in_specs=[pl.BlockSpec(memory_space=pltpu.VMEM)] * (len(blocks) + 1),
         out_specs=pl.BlockSpec(memory_space=pltpu.VMEM),
-        scratch_shapes=[
-            pltpu.VMEM((n + asked, flat), bf16),
-            pltpu.VMEM((n + asked, flat), bf16),
-            pltpu.VMEM((n + asked, flat), bf16),
-            pltpu.VMEM((asked, n), f32),
-        ],
+        scratch_shapes=[pltpu.VMEM((n + asked, n), f32)],
         compiler_params=pltpu.CompilerParams(vmem_limit_bytes=vmem_bytes),
         name="solve",
     )(*blocks, slots.reshape(1, asked))
@@ -219,12 +203,11 @@
 
 
 def gather_blocks(rows, size):
-    got = {0: rows, 8: flip(rows, 8, size)}
-    for k in (2, 4, 6):
-        got[k] = flip(rows, k, size)
-    for k in (2, 4, 6):
+    got = {0: rows, 8: flip(rows, 8, size), 2: flip(rows, 2, size), 4: flip(rows, 4, size)}
+    for k in (6, 4, 2):
         got[8 + k] = flip(got[8], k, size)
-    for k in range(0, size, 2):
+    got[6] = flip(got[4], 2, size)
+    for k in (0, 8, 2, 4, 6, 14, 12, 10):
         got[k + 1] = flip(got[k], 1, size)
     return [got[k] for k in range(size)]
 

time: 39.7 us -> 36.1 us (0.909)
  Pallas kernels: 19.4 us -> 15.1 us
  starting transfers between devices: 12.5 us -> 13.5 us
    pallas_call x1, Pallas kernels: 9.33 us -> 7.06 us  [project(): pl.pallas_call(functools.partial(project_kernel, size), out_shape=jax.Sha...]
    pallas_call x1, Pallas kernels: 10.1 us -> 7.99 us  [solve(): pl.pallas_call(functools.partial(solve_kernel, total, each, len(blocks)),...]
    ppermute x15, starting transfers between devices: 12.5 us -> 13.5 us  [flip(): return lax.ppermute(x, 'dp', [(i, i ^ bits) for i in range(size)])]
  transfers between devices with their start and end apart: 15 -> 15, of which waited for: 9 -> 7; matrix products, arithmetic and copies ran while one was open for 0% -> 0% of each run, Pallas kernels for 0% -> 0%
where the time goes in v2:
time: 36.1 us; the launch traced here: 36 us
  Pallas kernels  15.1 us (42%)
  starting transfers between devices  13.5 us (37%)
  waiting for transfers between devices  6.74 us (19%)
  local copies, waits for them, and re-layouts  0.57 us (2%)
    ppermute x15, starting transfers between devices, flip(): return lax.ppermute(x, 'dp', [(i, i ^ bits) for i in range(size)])  13.5 us
    pallas_call x1, Pallas kernels, solve(): pl.pallas_call(functools.partial(solve_kernel, total, each, len(blocks)),...  7.99 us
    pallas_call x1, Pallas kernels, project(): pl.pallas_call(functools.partial(project_kernel, size), out_shape=jax.Sha...  7.06 us
    ppermute x15, waiting for transfers between devices, flip(): return lax.ppermute(x, 'dp', [(i, i ^ bits) for i in range(size)])  6.74 us
  transfers between devices with their start and end apart: 15, of which 7 were waited for; matrix products, arithmetic and copies ran while one was open for 0% of the time, Pallas kernels for 0%

profile of v2, /device:TPU:0, one launch (start us, length us, event | category | flops | bytes accessed | tf_op | source)
XLA Modules:
  0.0 36.0 jit_solution(1158563400350079934)
XLA Ops:
  0.0 7.1 %project.1.refs_0_ = f32[24,1024]{1,0:T(8,128)} custom-call(bf16[16,16,14336]{2,1,0:T(8,128)(2,1)} %hidden.1, bf16[16,16,4096]{2,1,0:T(8,128)(2,1)} %grads.1, bf16[32,14336]{1,0:T(8,128)(2,1)} %pin.1, bf16[32,4096]{1,0:T(8,128)(2,1)} %pout.1, s32[16]{0:T(128)} %counts.1, f32[8,1024]{1,0:T(8,128)} %queries.1), custom_call_target="tpu_custom_call" | custom-call | tf_op jit(solution)/shard_map/project/pallas_call | solution.py:106
  7.1 4.1 %collective-permute-start.7 = (f32[24,1024]{1,0:T(8,128)}, f32[24,1024]{1,0:T(8,128)S(1)}, u32[]{:S(2)}, u32[]{:S(2)}) collective-permute-start(f32[24,1024]{1,0:T(8,128)} %project.1.refs_0_), channel_id=1, source_target_pairs={{0,8},{1,9},{2,10},{3,11},{4,12},{5,13},{6,14},{7,15},{8,0},{9,1},... | collective-permute-start | bytes 294920 | tf_op jit(solution)/shard_map/ppermute | solution.py:202
  11.2 1.6 %collective-permute-start.3 = (f32[24,1024]{1,0:T(8,128)}, f32[24,1024]{1,0:T(8,128)S(1)}, u32[]{:S(2)}, u32[]{:S(2)}) collective-permute-start(f32[24,1024]{1,0:T(8,128)} %project.1.refs_0_), channel_id=1, source_target_pairs={{0,4},{1,5},{2,6},{3,7},{4,0},{5,1},{6,2},{7,3},{8,12},{9,13},{10,... | collective-permute-start | bytes 294920 | tf_op jit(solution)/shard_map/ppermute | solution.py:202
  12.7 1.5 %collective-permute-start.1 = (f32[24,1024]{1,0:T(8,128)}, f32[24,1024]{1,0:T(8,128)S(1)}, u32[]{:S(2)}, u32[]{:S(2)}) collective-permute-start(f32[24,1024]{1,0:T(8,128)} %project.1.refs_0_), channel_id=1, source_target_pairs={{0,2},{1,3},{2,0},{3,1},{4,6},{5,7},{6,4},{7,5},{8,10},{9,11},{10,... | collective-permute-start | bytes 294920 | tf_op jit(solution)/shard_map/ppermute | solution.py:202
  14.3 0.0 collective-permute-start
  14.3 1.9 %collective-permute-done.7.refs_8_ = f32[24,1024]{1,0:T(8,128)S(1)} collective-permute-done((f32[24,1024]{1,0:T(8,128)}, f32[24,1024]{1,0:T(8,128)S(1)}, u32[]{:S(2)}, u32[]{:S(2)}) %collective-permute-start.7) | collective-permute-done | bytes 98336 | tf_op jit(solution)/shard_map/ppermute | solution.py:202
  16.1 1.9 %collective-permute-start.13 = (f32[24,1024]{1,0:T(8,128)S(1)}, f32[24,1024]{1,0:T(8,128)S(1)}, u32[]{:S(2)}, u32[]{:S(2)}) collective-permute-start(f32[24,1024]{1,0:T(8,128)S(1)} %collective-permute-done.7.refs_8_), channel_id=1, source_target_pairs={{0,6},{1,7},{2,4},{3,5},{4,2},{5,3},{6,0},{7,1},{8,14},{9,15},{10,... | collective-permute-start | bytes 294920 | tf_op jit(solution)/shard_map/ppermute | solution.py:202
  18.1 1.2 %collective-permute-start.11 = (f32[24,1024]{1,0:T(8,128)S(1)}, f32[24,1024]{1,0:T(8,128)S(1)}, u32[]{:S(2)}, u32[]{:S(2)}) collective-permute-start(f32[24,1024]{1,0:T(8,128)S(1)} %collective-permute-done.7.refs_8_), channel_id=1, source_target_pairs={{0,4},{1,5},{2,6},{3,7},{4,0},{5,1},{6,2},{7,3},{8,12},{9,13},{10,... | collective-permute-start | bytes 294920 | tf_op jit(solution)/shard_map/ppermute | solution.py:202
  19.3 0.0 collective-permute-done.3.refs_4_
  19.3 0.3 collective-permute-start.9
  19.6 0.0 collective-permute-done.1.refs_2_
  19.6 0.0 collective-permute-start.8
  19.6 0.0 collective-permute-done.refs_1_
  19.7 1.8 %collective-permute-start.5 = (f32[24,1024]{1,0:T(8,128)S(1)}, f32[24,1024]{1,0:T(8,128)S(1)}, u32[]{:S(2)}, u32[]{:S(2)}) collective-permute-start(f32[24,1024]{1,0:T(8,128)S(1)} %collective-permute-done.3.refs_4_), channel_id=1, source_target_pairs={{0,2},{1,3},{2,0},{3,1},{4,6},{5,7},{6,4},{7,5},{8,10},{9,11},{10,... | collective-permute-start | bytes 294920 | tf_op jit(solution)/shard_map/ppermute | solution.py:202
  21.4 1.1 %collective-permute-done.13.refs_14_ = f32[24,1024]{1,0:T(8,128)S(1)} collective-permute-done((f32[24,1024]{1,0:T(8,128)S(1)}, f32[24,1024]{1,0:T(8,128)S(1)}, u32[]{:S(2)}, u32[]{:S(2)}) %collective-permute-start.13) | collective-permute-done | bytes 98336 | tf_op jit(solution)/shard_map/ppermute | solution.py:202
  22.5 0.0 collective-permute-start.4
  22.5 1.0 %collective-permute-done.11.refs_12_ = f32[24,1024]{1,0:T(8,128)S(1)} collective-permute-done((f32[24,1024]{1,0:T(8,128)S(1)}, f32[24,1024]{1,0:T(8,128)S(1)}, u32[]{:S(2)}, u32[]{:S(2)}) %collective-permute-start.11) | collective-permute-done | bytes 98336 | tf_op jit(solution)/shard_map/ppermute | solution.py:202
  23.6 0.0 collective-permute-start.2
  23.6 1.3 %collective-permute-done.9.refs_10_ = f32[24,1024]{1,0:T(8,128)S(1)} collective-permute-done((f32[24,1024]{1,0:T(8,128)S(1)}, f32[24,1024]{1,0:T(8,128)S(1)}, u32[]{:S(2)}, u32[]{:S(2)}) %collective-permute-start.9) | collective-permute-done | bytes 98336 | tf_op jit(solution)/shard_map/ppermute | solution.py:202
  24.9 0.0 collective-permute-start.14
  24.9 0.0 collective-permute-done.8.refs_9_
  24.9 0.5 %collective-permute-start.12 = (f32[24,1024]{1,0:T(8,128)S(1)}, f32[24,1024]{1,0:T(8,128)S(1)}, u32[]{:S(2)}, u32[]{:S(2)}) collective-permute-start(f32[24,1024]{1,0:T(8,128)S(1)} %collective-permute-done.11.refs_12_), channel_id=1, source_target_pairs={{0,1},{1,0},{2,3},{3,2},{4,5},{5,4},{6,7},{7,6},{8,9},{9,8},{10,11... | collective-permute-start | bytes 294920 | tf_op jit(solution)/shard_map/ppermute | solution.py:202
  25.4 0.5 %collective-permute-done.5.refs_6_ = f32[24,1024]{1,0:T(8,128)S(1)} collective-permute-done((f32[24,1024]{1,0:T(8,128)S(1)}, f32[24,1024]{1,0:T(8,128)S(1)}, u32[]{:S(2)}, u32[]{:S(2)}) %collective-permute-start.5) | collective-permute-done | bytes 98336 | tf_op jit(solution)/shard_map/ppermute | solution.py:202
  25.9 0.0 collective-permute-start.10
  25.9 0.0 collective-permute-done.4.refs_5_
  25.9 0.5 %collective-permute-start.6 = (f32[24,1024]{1,0:T(8,128)S(1)}, f32[24,1024]{1,0:T(8,128)S(1)}, u32[]{:S(2)}, u32[]{:S(2)}) collective-permute-start(f32[24,1024]{1,0:T(8,128)S(1)} %collective-permute-done.5.refs_6_), channel_id=1, source_target_pairs={{0,1},{1,0},{2,3},{3,2},{4,5},{5,4},{6,7},{7,6},{8,9},{9,8},{10,11... | collective-permute-start | bytes 294920 | tf_op jit(solution)/shard_map/ppermute | solution.py:202
  26.5 0.0 collective-permute-done.12.refs_13_
  26.5 0.7 %collective-permute-done.10.refs_11_ = f32[24,1024]{1,0:T(8,128)S(1)} collective-permute-done((f32[24,1024]{1,0:T(8,128)S(1)}, f32[24,1024]{1,0:T(8,128)S(1)}, u32[]{:S(2)}, u32[]{:S(2)}) %collective-permute-start.10) | collective-permute-done | bytes 98336 | tf_op jit(solution)/shard_map/ppermute | solution.py:202
  27.2 0.2 collective-permute-done.6.refs_7_
  27.5 0.4 copy-done.13
  27.8 0.2 copy-done.14
  28.0 8.0 %solve.1 = f32[16,128]{1,0:T(8,128)} custom-call(f32[24,1024]{1,0:T(8,128)} %project.1.refs_0_, f32[24,1024]{1,0:T(8,128)} %copy-done.3, f32[24,1024]{1,0:T(8,128)} %copy-done.2, f32[24,1024]{1,0:T(8,128)} %copy-done.10, f32[24,1024]{1,0:T(8,128)} %copy-done.1, f32[24,1024]{1,0:T(8,128)} %copy-done.9, f32[24,1024]{1,0:T(8,128)} %copy-done.8, ...), custom_call_target="tpu_custom_call" | custom-call | tf_op jit(solution)/shard_map/solve/pallas_call | solution.py:190
  (30 shorter events, 0.1 us)
Async XLA Ops:
  7.1 9.1 %collective-permute-start.7 = (f32[24,1024]{1,0:T(8,128)}, f32[24,1024]{1,0:T(8,128)S(1)}, u32[]{:S(2)}, u32[]{:S(2)}) collective-permute-start(f32[24,1024]{1,0:T(8,128)} %project.1.refs_0_), channel_id=1, source_target_pairs={{0,8},{1,9},{2,10},{3,11},{4,12},{5,13},{6,14},{7,15},{8,0},{9,1},... | collective-permute-start | bytes 294920 | tf_op jit(solution)/shard_map/ppermute | solution.py:202
  11.2 8.2 %collective-permute-start.3 = (f32[24,1024]{1,0:T(8,128)}, f32[24,1024]{1,0:T(8,128)S(1)}, u32[]{:S(2)}, u32[]{:S(2)}) collective-permute-start(f32[24,1024]{1,0:T(8,128)} %project.1.refs_0_), channel_id=1, source_target_pairs={{0,4},{1,5},{2,6},{3,7},{4,0},{5,1},{6,2},{7,3},{8,12},{9,13},{10,... | collective-permute-start | bytes 294920 | tf_op jit(solution)/shard_map/ppermute | solution.py:202
  12.7 6.9 %collective-permute-start.1 = (f32[24,1024]{1,0:T(8,128)}, f32[24,1024]{1,0:T(8,128)S(1)}, u32[]{:S(2)}, u32[]{:S(2)}) collective-permute-start(f32[24,1024]{1,0:T(8,128)} %project.1.refs_0_), channel_id=1, source_target_pairs={{0,2},{1,3},{2,0},{3,1},{4,6},{5,7},{6,4},{7,5},{8,10},{9,11},{10,... | collective-permute-start | bytes 294920 | tf_op jit(solution)/shard_map/ppermute | solution.py:202
  14.3 5.4 %collective-permute-start = (f32[24,1024]{1,0:T(8,128)}, f32[24,1024]{1,0:T(8,128)S(1)}, u32[]{:S(2)}, u32[]{:S(2)}) collective-permute-start(f32[24,1024]{1,0:T(8,128)} %project.1.refs_0_), channel_id=1, source_target_pairs={{0,1},{1,0},{2,3},{3,2},{4,5},{5,4},{6,7},{7,6},{8,9},{9,8},{10,11... | collective-permute-start | bytes 294920 | tf_op jit(solution)/shard_map/ppermute | solution.py:202
  16.1 11.3 %copy-start = (f32[24,1024]{1,0:T(8,128)}, f32[24,1024]{1,0:T(8,128)S(1)}, u32[]{:S(2)}) copy-start(f32[24,1024]{1,0:T(8,128)S(1)} %collective-permute-done.7.refs_8_) | copy-start | bytes 294916
  16.1 6.4 %collective-permute-start.13 = (f32[24,1024]{1,0:T(8,128)S(1)}, f32[24,1024]{1,0:T(8,128)S(1)}, u32[]{:S(2)}, u32[]{:S(2)}) collective-permute-start(f32[24,1024]{1,0:T(8,128)S(1)} %collective-permute-done.7.refs_8_), channel_id=1, source_target_pairs={{0,6},{1,7},{2,4},{3,5},{4,2},{5,3},{6,0},{7,1},{8,14},{9,15},{10,... | collective-permute-start | bytes 294920 | tf_op jit(solution)/shard_map/ppermute | solution.py:202
  18.1 5.5 %collective-permute-start.11 = (f32[24,1024]{1,0:T(8,128)S(1)}, f32[24,1024]{1,0:T(8,128)S(1)}, u32[]{:S(2)}, u32[]{:S(2)}) collective-permute-start(f32[24,1024]{1,0:T(8,128)S(1)} %collective-permute-done.7.refs_8_), channel_id=1, source_target_pairs={{0,4},{1,5},{2,6},{3,7},{4,0},{5,1},{6,2},{7,3},{8,12},{9,13},{10,... | collective-permute-start | bytes 294920 | tf_op jit(solution)/shard_map/ppermute | solution.py:202
  19.3 8.1 %copy-start.1 = (f32[24,1024]{1,0:T(8,128)}, f32[24,1024]{1,0:T(8,128)S(1)}, u32[]{:S(2)}) copy-start(f32[24,1024]{1,0:T(8,128)S(1)} %collective-permute-done.3.refs_4_) | copy-start | bytes 294916
  19.3 5.5 %collective-permute-start.9 = (f32[24,1024]{1,0:T(8,128)S(1)}, f32[24,1024]{1,0:T(8,128)S(1)}, u32[]{:S(2)}, u32[]{:S(2)}) collective-permute-start(f32[24,1024]{1,0:T(8,128)S(1)} %collective-permute-done.7.refs_8_), channel_id=1, source_target_pairs={{0,2},{1,3},{2,0},{3,1},{4,6},{5,7},{6,4},{7,5},{8,10},{9,11},{10,... | collective-permute-start | bytes 294920 | tf_op jit(solution)/shard_map/ppermute | solution.py:202
  19.6 7.8 %copy-start.2 = (f32[24,1024]{1,0:T(8,128)}, f32[24,1024]{1,0:T(8,128)S(1)}, u32[]{:S(2)}) copy-start(f32[24,1024]{1,0:T(8,128)S(1)} %collective-permute-done.1.refs_2_) | copy-start | bytes 294916
  19.6 5.2 %collective-permute-start.8 = (f32[24,1024]{1,0:T(8,128)S(1)}, f32[24,1024]{1,0:T(8,128)S(1)}, u32[]{:S(2)}, u32[]{:S(2)}) collective-permute-start(f32[24,1024]{1,0:T(8,128)S(1)} %collective-permute-done.7.refs_8_), channel_id=1, source_target_pairs={{0,1},{1,0},{2,3},{3,2},{4,5},{5,4},{6,7},{7,6},{8,9},{9,8},{10,11... | collective-permute-start | bytes 294920 | tf_op jit(solution)/shard_map/ppermute | solution.py:202
  19.6 7.7 %copy-start.3 = (f32[24,1024]{1,0:T(8,128)}, f32[24,1024]{1,0:T(8,128)S(1)}, u32[]{:S(2)}) copy-start(f32[24,1024]{1,0:T(8,128)S(1)} %collective-permute-done.refs_1_) | copy-start | bytes 294916
  19.7 6.3 %collective-permute-start.5 = (f32[24,1024]{1,0:T(8,128)S(1)}, f32[24,1024]{1,0:T(8,128)S(1)}, u32[]{:S(2)}, u32[]{:S(2)}) collective-permute-start(f32[24,1024]{1,0:T(8,128)S(1)} %collective-permute-done.3.refs_4_), channel_id=1, source_target_pairs={{0,2},{1,3},{2,0},{3,1},{4,6},{5,7},{6,4},{7,5},{8,10},{9,11},{10,... | collective-permute-start | bytes 294920 | tf_op jit(solution)/shard_map/ppermute | solution.py:202
  22.5 4.9 %copy-start.4 = (f32[24,1024]{1,0:T(8,128)}, f32[24,1024]{1,0:T(8,128)S(1)}, u32[]{:S(2)}) copy-start(f32[24,1024]{1,0:T(8,128)S(1)} %collective-permute-done.13.refs_14_) | copy-start | bytes 294916
  22.5 3.4 %collective-permute-start.4 = (f32[24,1024]{1,0:T(8,128)S(1)}, f32[24,1024]{1,0:T(8,128)S(1)}, u32[]{:S(2)}, u32[]{:S(2)}) collective-permute-start(f32[24,1024]{1,0:T(8,128)S(1)} %collective-permute-done.3.refs_4_), channel_id=1, source_target_pairs={{0,1},{1,0},{2,3},{3,2},{4,5},{5,4},{6,7},{7,6},{8,9},{9,8},{10,11... | collective-permute-start | bytes 294920 | tf_op jit(solution)/shard_map/ppermute | solution.py:202
  23.6 3.9 %copy-start.5 = (f32[24,1024]{1,0:T(8,128)}, f32[24,1024]{1,0:T(8,128)S(1)}, u32[]{:S(2)}) copy-start(f32[24,1024]{1,0:T(8,128)S(1)} %collective-permute-done.11.refs_12_) | copy-start | bytes 294916
  23.6 2.9 %collective-permute-start.2 = (f32[24,1024]{1,0:T(8,128)S(1)}, f32[24,1024]{1,0:T(8,128)S(1)}, u32[]{:S(2)}, u32[]{:S(2)}) collective-permute-start(f32[24,1024]{1,0:T(8,128)S(1)} %collective-permute-done.1.refs_2_), channel_id=1, source_target_pairs={{0,1},{1,0},{2,3},{3,2},{4,5},{5,4},{6,7},{7,6},{8,9},{9,8},{10,11... | collective-permute-start | bytes 294920 | tf_op jit(solution)/shard_map/ppermute | solution.py:202
  24.9 2.6 %copy-start.6 = (f32[24,1024]{1,0:T(8,128)}, f32[24,1024]{1,0:T(8,128)S(1)}, u32[]{:S(2)}) copy-start(f32[24,1024]{1,0:T(8,128)S(1)} %collective-permute-done.9.refs_10_) | copy-start | bytes 294916
  24.9 1.6 %collective-permute-start.14 = (f32[24,1024]{1,0:T(8,128)S(1)}, f32[24,1024]{1,0:T(8,128)S(1)}, u32[]{:S(2)}, u32[]{:S(2)}) collective-permute-start(f32[24,1024]{1,0:T(8,128)S(1)} %collective-permute-done.13.refs_14_), channel_id=1, source_target_pairs={{0,1},{1,0},{2,3},{3,2},{4,5},{5,4},{6,7},{7,6},{8,9},{9,8},{10,11... | collective-permute-start | bytes 294920 | tf_op jit(solution)/shard_map/ppermute | solution.py:202
  24.9 2.6 %copy-start.7 = (f32[24,1024]{1,0:T(8,128)}, f32[24,1024]{1,0:T(8,128)S(1)}, u32[]{:S(2)}) copy-start(f32[24,1024]{1,0:T(8,128)S(1)} %collective-permute-done.8.refs_9_) | copy-start | bytes 294916
  24.9 1.6 %collective-permute-start.12 = (f32[24,1024]{1,0:T(8,128)S(1)}, f32[24,1024]{1,0:T(8,128)S(1)}, u32[]{:S(2)}, u32[]{:S(2)}) collective-permute-start(f32[24,1024]{1,0:T(8,128)S(1)} %collective-permute-done.11.refs_12_), channel_id=1, source_target_pairs={{0,1},{1,0},{2,3},{3,2},{4,5},{5,4},{6,7},{7,6},{8,9},{9,8},{10,11... | collective-permute-start | bytes 294920 | tf_op jit(solution)/shard_map/ppermute | solution.py:202
  25.9 1.5 %copy-start.8 = (f32[24,1024]{1,0:T(8,128)}, f32[24,1024]{1,0:T(8,128)S(1)}, u32[]{:S(2)}) copy-start(f32[24,1024]{1,0:T(8,128)S(1)} %collective-permute-done.5.refs_6_) | copy-start | bytes 294916
  25.9 1.3 %collective-permute-start.10 = (f32[24,1024]{1,0:T(8,128)S(1)}, f32[24,1024]{1,0:T(8,128)S(1)}, u32[]{:S(2)}, u32[]{:S(2)}) collective-permute-start(f32[24,1024]{1,0:T(8,128)S(1)} %collective-permute-done.9.refs_10_), channel_id=1, source_target_pairs={{0,1},{1,0},{2,3},{3,2},{4,5},{5,4},{6,7},{7,6},{8,9},{9,8},{10,11... | collective-permute-start | bytes 294920 | tf_op jit(solution)/shard_map/ppermute | solution.py:202
  25.9 1.5 %copy-start.9 = (f32[24,1024]{1,0:T(8,128)}, f32[24,1024]{1,0:T(8,128)S(1)}, u32[]{:S(2)}) copy-start(f32[24,1024]{1,0:T(8,128)S(1)} %collective-permute-done.4.refs_5_) | copy-start | bytes 294916
  25.9 1.4 %collective-permute-start.6 = (f32[24,1024]{1,0:T(8,128)S(1)}, f32[24,1024]{1,0:T(8,128)S(1)}, u32[]{:S(2)}, u32[]{:S(2)}) collective-permute-start(f32[24,1024]{1,0:T(8,128)S(1)} %collective-permute-done.5.refs_6_), channel_id=1, source_target_pairs={{0,1},{1,0},{2,3},{3,2},{4,5},{5,4},{6,7},{7,6},{8,9},{9,8},{10,11... | collective-permute-start | bytes 294920 | tf_op jit(solution)/shard_map/ppermute | solution.py:202
  26.4 1.0 %copy-start.10 = (f32[24,1024]{1,0:T(8,128)}, f32[24,1024]{1,0:T(8,128)S(1)}, u32[]{:S(2)}) copy-start(f32[24,1024]{1,0:T(8,128)S(1)} %collective-permute-done.2.refs_3_) | copy-start | bytes 294916
  26.4 1.0 %copy-start.11 = (f32[24,1024]{1,0:T(8,128)}, f32[24,1024]{1,0:T(8,128)S(1)}, u32[]{:S(2)}) copy-start(f32[24,1024]{1,0:T(8,128)S(1)} %collective-permute-done.14.refs_15_) | copy-start | bytes 294916
  26.5 1.0 %copy-start.12 = (f32[24,1024]{1,0:T(8,128)}, f32[24,1024]{1,0:T(8,128)S(1)}, u32[]{:S(2)}) copy-start(f32[24,1024]{1,0:T(8,128)S(1)} %collective-permute-done.12.refs_13_) | copy-start | bytes 294916
  27.2 0.6 %copy-start.13 = (f32[24,1024]{1,0:T(8,128)}, f32[24,1024]{1,0:T(8,128)S(1)}, u32[]{:S(2)}) copy-start(f32[24,1024]{1,0:T(8,128)S(1)} %collective-permute-done.10.refs_11_) | copy-start | bytes 294916
  27.4 0.6 %copy-start.14 = (f32[24,1024]{1,0:T(8,128)}, f32[24,1024]{1,0:T(8,128)S(1)}, u32[]{:S(2)}) copy-start(f32[24,1024]{1,0:T(8,128)S(1)} %collective-permute-done.6.refs_7_) | copy-start | bytes 294916

commit v3 on v2

--- a/solution.py
+++ b/solution.py
@@ -203,11 +203,12 @@
 
 
 def gather_blocks(rows, size):
-    got = {0: rows, 8: flip(rows, 8, size), 2: flip(rows, 2, size), 4: flip(rows, 4, size)}
+    got = {0: rows}
+    for k in (8, 6, 4, 2):
+        got[k] = flip(rows, k, size)
     for k in (6, 4, 2):
         got[8 + k] = flip(got[8], k, size)
-    got[6] = flip(got[4], 2, size)
-    for k in (0, 8, 2, 4, 6, 14, 12, 10):
+    for k in (0, 8, 2, 4, 6, 10, 12, 14):
         got[k + 1] = flip(got[k], 1, size)
     return [got[k] for k in range(size)]
 

time: 36.1 us -> 35.4 us (0.981)
  starting transfers between devices: 13.5 us -> 12.5 us
    ppermute x15, starting transfers between devices: 13.5 us -> 12.5 us  [flip(): return lax.ppermute(x, 'dp', [(i, i ^ bits) for i in range(size)])]
  transfers between devices with their start and end apart: 15 -> 15, of which waited for: 7 -> 9; matrix products, arithmetic and copies ran while one was open for 0% -> 0% of each run, Pallas kernels for 0% -> 0%
where the time goes in v3:
time: 35.4 us
  Pallas kernels  15 us (42%)
  starting transfers between devices  12.5 us (35%)
  waiting for transfers between devices  7.06 us (20%)
  local copies, waits for them, and re-layouts  0.57 us (2%)
    ppermute x15, starting transfers between devices, flip(): return lax.ppermute(x, 'dp', [(i, i ^ bits) for i in range(size)])  12.5 us
    pallas_call x1, Pallas kernels, solve(): pl.pallas_call(functools.partial(solve_kernel, total, each, len(blocks)),...  7.99 us
    pallas_call x1, Pallas kernels, project(): pl.pallas_call(functools.partial(project_kernel, size), out_shape=jax.Sha...  7.06 us
    ppermute x15, waiting for transfers between devices, flip(): return lax.ppermute(x, 'dp', [(i, i ^ bits) for i in range(size)])  7.06 us
  transfers between devices with their start and end apart: 15, of which 9 were waited for; matrix products, arithmetic and copies ran while one was open for 0% of the time, Pallas kernels for 0%

profile of v3, /device:TPU:0, one launch (start us, length us, event | category | flops | bytes accessed | tf_op | source)
XLA Modules:
  0.0 35.4 jit_solution(1815977965432696599)
XLA Ops:
  0.0 7.1 %project.1.refs_0_ = f32[24,1024]{1,0:T(8,128)} custom-call(bf16[16,16,14336]{2,1,0:T(8,128)(2,1)} %hidden.1, bf16[16,16,4096]{2,1,0:T(8,128)(2,1)} %grads.1, bf16[32,14336]{1,0:T(8,128)(2,1)} %pin.1, bf16[32,4096]{1,0:T(8,128)(2,1)} %pout.1, s32[16]{0:T(128)} %counts.1, f32[8,1024]{1,0:T(8,128)} %queries.1), custom_call_target="tpu_custom_call" | custom-call | tf_op jit(solution)/shard_map/project/pallas_call | solution.py:106
  7.1 4.1 %collective-permute-start.7 = (f32[24,1024]{1,0:T(8,128)}, f32[24,1024]{1,0:T(8,128)S(1)}, u32[]{:S(2)}, u32[]{:S(2)}) collective-permute-start(f32[24,1024]{1,0:T(8,128)} %project.1.refs_0_), channel_id=1, source_target_pairs={{0,8},{1,9},{2,10},{3,11},{4,12},{5,13},{6,14},{7,15},{8,0},{9,1},... | collective-permute-start | bytes 294920 | tf_op jit(solution)/shard_map/ppermute | solution.py:202
  11.2 2.5 %collective-permute-start.5 = (f32[24,1024]{1,0:T(8,128)}, f32[24,1024]{1,0:T(8,128)S(1)}, u32[]{:S(2)}, u32[]{:S(2)}) collective-permute-start(f32[24,1024]{1,0:T(8,128)} %project.1.refs_0_), channel_id=1, source_target_pairs={{0,6},{1,7},{2,4},{3,5},{4,2},{5,3},{6,0},{7,1},{8,14},{9,15},{10,... | collective-permute-start | bytes 294920 | tf_op jit(solution)/shard_map/ppermute | solution.py:202
  13.7 0.5 %collective-permute-start.3 = (f32[24,1024]{1,0:T(8,128)}, f32[24,1024]{1,0:T(8,128)S(1)}, u32[]{:S(2)}, u32[]{:S(2)}) collective-permute-start(f32[24,1024]{1,0:T(8,128)} %project.1.refs_0_), channel_id=1, source_target_pairs={{0,4},{1,5},{2,6},{3,7},{4,0},{5,1},{6,2},{7,3},{8,12},{9,13},{10,... | collective-permute-start | bytes 294920 | tf_op jit(solution)/shard_map/ppermute | solution.py:202
  14.2 0.5 %collective-permute-start.1 = (f32[24,1024]{1,0:T(8,128)}, f32[24,1024]{1,0:T(8,128)S(1)}, u32[]{:S(2)}, u32[]{:S(2)}) collective-permute-start(f32[24,1024]{1,0:T(8,128)} %project.1.refs_0_), channel_id=1, source_target_pairs={{0,2},{1,3},{2,0},{3,1},{4,6},{5,7},{6,4},{7,5},{8,10},{9,11},{10,... | collective-permute-start | bytes 294920 | tf_op jit(solution)/shard_map/ppermute | solution.py:202
  14.6 0.0 collective-permute-start
  14.6 1.5 %collective-permute-done.7.refs_8_ = f32[24,1024]{1,0:T(8,128)S(1)} collective-permute-done((f32[24,1024]{1,0:T(8,128)}, f32[24,1024]{1,0:T(8,128)S(1)}, u32[]{:S(2)}, u32[]{:S(2)}) %collective-permute-start.7) | collective-permute-done | bytes 98336 | tf_op jit(solution)/shard_map/ppermute | solution.py:202
  16.2 2.0 %collective-permute-start.13 = (f32[24,1024]{1,0:T(8,128)S(1)}, f32[24,1024]{1,0:T(8,128)S(1)}, u32[]{:S(2)}, u32[]{:S(2)}) collective-permute-start(f32[24,1024]{1,0:T(8,128)S(1)} %collective-permute-done.7.refs_8_), channel_id=1, source_target_pairs={{0,6},{1,7},{2,4},{3,5},{4,2},{5,3},{6,0},{7,1},{8,14},{9,15},{10,... | collective-permute-start | bytes 294920 | tf_op jit(solution)/shard_map/ppermute | solution.py:202
  18.1 0.6 %collective-permute-done.5.refs_6_ = f32[24,1024]{1,0:T(8,128)S(1)} collective-permute-done((f32[24,1024]{1,0:T(8,128)}, f32[24,1024]{1,0:T(8,128)S(1)}, u32[]{:S(2)}, u32[]{:S(2)}) %collective-permute-start.5) | collective-permute-done | bytes 98336 | tf_op jit(solution)/shard_map/ppermute | solution.py:202
  18.7 1.3 %collective-permute-start.11 = (f32[24,1024]{1,0:T(8,128)S(1)}, f32[24,1024]{1,0:T(8,128)S(1)}, u32[]{:S(2)}, u32[]{:S(2)}) collective-permute-start(f32[24,1024]{1,0:T(8,128)S(1)} %collective-permute-done.7.refs_8_), channel_id=1, source_target_pairs={{0,4},{1,5},{2,6},{3,7},{4,0},{5,1},{6,2},{7,3},{8,12},{9,13},{10,... | collective-permute-start | bytes 294920 | tf_op jit(solution)/shard_map/ppermute | solution.py:202
  20.0 0.3 collective-permute-done.3.refs_4_
  20.3 0.6 %collective-permute-start.9 = (f32[24,1024]{1,0:T(8,128)S(1)}, f32[24,1024]{1,0:T(8,128)S(1)}, u32[]{:S(2)}, u32[]{:S(2)}) collective-permute-start(f32[24,1024]{1,0:T(8,128)S(1)} %collective-permute-done.7.refs_8_), channel_id=1, source_target_pairs={{0,2},{1,3},{2,0},{3,1},{4,6},{5,7},{6,4},{7,5},{8,10},{9,11},{10,... | collective-permute-start | bytes 294920 | tf_op jit(solution)/shard_map/ppermute | solution.py:202
  20.9 0.0 collective-permute-done.1.refs_2_
  20.9 0.0 collective-permute-start.8
  20.9 0.0 collective-permute-done.refs_1_
  20.9 0.5 %collective-permute-start.6 = (f32[24,1024]{1,0:T(8,128)S(1)}, f32[24,1024]{1,0:T(8,128)S(1)}, u32[]{:S(2)}, u32[]{:S(2)}) collective-permute-start(f32[24,1024]{1,0:T(8,128)S(1)} %collective-permute-done.5.refs_6_), channel_id=1, source_target_pairs={{0,1},{1,0},{2,3},{3,2},{4,5},{5,4},{6,7},{7,6},{8,9},{9,8},{10,11... | collective-permute-start | bytes 294920 | tf_op jit(solution)/shard_map/ppermute | solution.py:202
  21.4 1.4 %collective-permute-done.13.refs_14_ = f32[24,1024]{1,0:T(8,128)S(1)} collective-permute-done((f32[24,1024]{1,0:T(8,128)S(1)}, f32[24,1024]{1,0:T(8,128)S(1)}, u32[]{:S(2)}, u32[]{:S(2)}) %collective-permute-start.13) | collective-permute-done | bytes 98336 | tf_op jit(solution)/shard_map/ppermute | solution.py:202
  22.8 0.0 collective-permute-start.4
  22.8 1.0 %collective-permute-done.11.refs_12_ = f32[24,1024]{1,0:T(8,128)S(1)} collective-permute-done((f32[24,1024]{1,0:T(8,128)S(1)}, f32[24,1024]{1,0:T(8,128)S(1)}, u32[]{:S(2)}, u32[]{:S(2)}) %collective-permute-start.11) | collective-permute-done | bytes 98336 | tf_op jit(solution)/shard_map/ppermute | solution.py:202
  23.7 0.0 collective-permute-start.2
  23.7 1.2 %collective-permute-done.9.refs_10_ = f32[24,1024]{1,0:T(8,128)S(1)} collective-permute-done((f32[24,1024]{1,0:T(8,128)S(1)}, f32[24,1024]{1,0:T(8,128)S(1)}, u32[]{:S(2)}, u32[]{:S(2)}) %collective-permute-start.9) | collective-permute-done | bytes 98336 | tf_op jit(solution)/shard_map/ppermute | solution.py:202
  24.9 0.0 collective-permute-start.14
  24.9 0.5 %collective-permute-start.12 = (f32[24,1024]{1,0:T(8,128)S(1)}, f32[24,1024]{1,0:T(8,128)S(1)}, u32[]{:S(2)}, u32[]{:S(2)}) collective-permute-start(f32[24,1024]{1,0:T(8,128)S(1)} %collective-permute-done.11.refs_12_), channel_id=1, source_target_pairs={{0,1},{1,0},{2,3},{3,2},{4,5},{5,4},{6,7},{7,6},{8,9},{9,8},{10,11... | collective-permute-start | bytes 294920 | tf_op jit(solution)/shard_map/ppermute | solution.py:202
  25.4 0.1 collective-permute-start.10
  25.5 0.0 collective-permute-done.4.refs_5_
  25.5 0.7 %collective-permute-done.14.refs_15_ = f32[24,1024]{1,0:T(8,128)S(1)} collective-permute-done((f32[24,1024]{1,0:T(8,128)S(1)}, f32[24,1024]{1,0:T(8,128)S(1)}, u32[]{:S(2)}, u32[]{:S(2)}) %collective-permute-start.14) | collective-permute-done | bytes 98336 | tf_op jit(solution)/shard_map/ppermute | solution.py:202
  26.2 0.2 collective-permute-done.12.refs_13_
  26.4 0.4 %collective-permute-done.10.refs_11_ = f32[24,1024]{1,0:T(8,128)S(1)} collective-permute-done((f32[24,1024]{1,0:T(8,128)S(1)}, f32[24,1024]{1,0:T(8,128)S(1)}, u32[]{:S(2)}, u32[]{:S(2)}) %collective-permute-start.10) | collective-permute-done | bytes 98336 | tf_op jit(solution)/shard_map/ppermute | solution.py:202
  26.8 0.0 copy-done.12
  26.8 0.2 copy-done.13
  27.0 0.4 copy-done.14
  27.4 8.0 %solve.1 = f32[16,128]{1,0:T(8,128)} custom-call(f32[24,1024]{1,0:T(8,128)} %project.1.refs_0_, f32[24,1024]{1,0:T(8,128)} %copy-done.4, f32[24,1024]{1,0:T(8,128)} %copy-done.3, f32[24,1024]{1,0:T(8,128)} %copy-done.11, f32[24,1024]{1,0:T(8,128)} %copy-done.2, f32[24,1024]{1,0:T(8,128)} %copy-done.10, f32[24,1024]{1,0:T(8,128)} %copy-done.1, ...), custom_call_target="tpu_custom_call" | custom-call | tf_op jit(solution)/shard_map/solve/pallas_call | solution.py:190
  (30 shorter events, 0.1 us)
Async XLA Ops:
  7.1 9.1 %collective-permute-start.7 = (f32[24,1024]{1,0:T(8,128)}, f32[24,1024]{1,0:T(8,128)S(1)}, u32[]{:S(2)}, u32[]{:S(2)}) collective-permute-start(f32[24,1024]{1,0:T(8,128)} %project.1.refs_0_), channel_id=1, source_target_pairs={{0,8},{1,9},{2,10},{3,11},{4,12},{5,13},{6,14},{7,15},{8,0},{9,1},... | collective-permute-start | bytes 294920 | tf_op jit(solution)/shard_map/ppermute | solution.py:202
  11.2 7.6 %collective-permute-start.5 = (f32[24,1024]{1,0:T(8,128)}, f32[24,1024]{1,0:T(8,128)S(1)}, u32[]{:S(2)}, u32[]{:S(2)}) collective-permute-start(f32[24,1024]{1,0:T(8,128)} %project.1.refs_0_), channel_id=1, source_target_pairs={{0,6},{1,7},{2,4},{3,5},{4,2},{5,3},{6,0},{7,1},{8,14},{9,15},{10,... | collective-permute-start | bytes 294920 | tf_op jit(solution)/shard_map/ppermute | solution.py:202
  13.7 6.6 %collective-permute-start.3 = (f32[24,1024]{1,0:T(8,128)}, f32[24,1024]{1,0:T(8,128)S(1)}, u32[]{:S(2)}, u32[]{:S(2)}) collective-permute-start(f32[24,1024]{1,0:T(8,128)} %project.1.refs_0_), channel_id=1, source_target_pairs={{0,4},{1,5},{2,6},{3,7},{4,0},{5,1},{6,2},{7,3},{8,12},{9,13},{10,... | collective-permute-start | bytes 294920 | tf_op jit(solution)/shard_map/ppermute | solution.py:202
  14.2 6.7 %collective-permute-start.1 = (f32[24,1024]{1,0:T(8,128)}, f32[24,1024]{1,0:T(8,128)S(1)}, u32[]{:S(2)}, u32[]{:S(2)}) collective-permute-start(f32[24,1024]{1,0:T(8,128)} %project.1.refs_0_), channel_id=1, source_target_pairs={{0,2},{1,3},{2,0},{3,1},{4,6},{5,7},{6,4},{7,5},{8,10},{9,11},{10,... | collective-permute-start | bytes 294920 | tf_op jit(solution)/shard_map/ppermute | solution.py:202
  14.6 6.2 %collective-permute-start = (f32[24,1024]{1,0:T(8,128)}, f32[24,1024]{1,0:T(8,128)S(1)}, u32[]{:S(2)}, u32[]{:S(2)}) collective-permute-start(f32[24,1024]{1,0:T(8,128)} %project.1.refs_0_), channel_id=1, source_target_pairs={{0,1},{1,0},{2,3},{3,2},{4,5},{5,4},{6,7},{7,6},{8,9},{9,8},{10,11... | collective-permute-start | bytes 294920 | tf_op jit(solution)/shard_map/ppermute | solution.py:202
  16.2 10.6 %copy-start = (f32[24,1024]{1,0:T(8,128)}, f32[24,1024]{1,0:T(8,128)S(1)}, u32[]{:S(2)}) copy-start(f32[24,1024]{1,0:T(8,128)S(1)} %collective-permute-done.7.refs_8_) | copy-start | bytes 294916
  16.2 6.6 %collective-permute-start.13 = (f32[24,1024]{1,0:T(8,128)S(1)}, f32[24,1024]{1,0:T(8,128)S(1)}, u32[]{:S(2)}, u32[]{:S(2)}) collective-permute-start(f32[24,1024]{1,0:T(8,128)S(1)} %collective-permute-done.7.refs_8_), channel_id=1, source_target_pairs={{0,6},{1,7},{2,4},{3,5},{4,2},{5,3},{6,0},{7,1},{8,14},{9,15},{10,... | collective-permute-start | bytes 294920 | tf_op jit(solution)/shard_map/ppermute | solution.py:202
  18.7 8.0 %copy-start.1 = (f32[24,1024]{1,0:T(8,128)}, f32[24,1024]{1,0:T(8,128)S(1)}, u32[]{:S(2)}) copy-start(f32[24,1024]{1,0:T(8,128)S(1)} %collective-permute-done.5.refs_6_) | copy-start | bytes 294916
  18.7 5.0 %collective-permute-start.11 = (f32[24,1024]{1,0:T(8,128)S(1)}, f32[24,1024]{1,0:T(8,128)S(1)}, u32[]{:S(2)}, u32[]{:S(2)}) collective-permute-start(f32[24,1024]{1,0:T(8,128)S(1)} %collective-permute-done.7.refs_8_), channel_id=1, source_target_pairs={{0,4},{1,5},{2,6},{3,7},{4,0},{5,1},{6,2},{7,3},{8,12},{9,13},{10,... | collective-permute-start | bytes 294920 | tf_op jit(solution)/shard_map/ppermute | solution.py:202
  20.3 6.5 %copy-start.2 = (f32[24,1024]{1,0:T(8,128)}, f32[24,1024]{1,0:T(8,128)S(1)}, u32[]{:S(2)}) copy-start(f32[24,1024]{1,0:T(8,128)S(1)} %collective-permute-done.3.refs_4_) | copy-start | bytes 294916
  20.3 4.6 %collective-permute-start.9 = (f32[24,1024]{1,0:T(8,128)S(1)}, f32[24,1024]{1,0:T(8,128)S(1)}, u32[]{:S(2)}, u32[]{:S(2)}) collective-permute-start(f32[24,1024]{1,0:T(8,128)S(1)} %collective-permute-done.7.refs_8_), channel_id=1, source_target_pairs={{0,2},{1,3},{2,0},{3,1},{4,6},{5,7},{6,4},{7,5},{8,10},{9,11},{10,... | collective-permute-start | bytes 294920 | tf_op jit(solution)/shard_map/ppermute | solution.py:202
  20.9 5.9 %copy-start.3 = (f32[24,1024]{1,0:T(8,128)}, f32[24,1024]{1,0:T(8,128)S(1)}, u32[]{:S(2)}) copy-start(f32[24,1024]{1,0:T(8,128)S(1)} %collective-permute-done.1.refs_2_) | copy-start | bytes 294916
  20.9 4.0 %collective-permute-start.8 = (f32[24,1024]{1,0:T(8,128)S(1)}, f32[24,1024]{1,0:T(8,128)S(1)}, u32[]{:S(2)}, u32[]{:S(2)}) collective-permute-start(f32[24,1024]{1,0:T(8,128)S(1)} %collective-permute-done.7.refs_8_), channel_id=1, source_target_pairs={{0,1},{1,0},{2,3},{3,2},{4,5},{5,4},{6,7},{7,6},{8,9},{9,8},{10,11... | collective-permute-start | bytes 294920 | tf_op jit(solution)/shard_map/ppermute | solution.py:202
  20.9 5.9 %copy-start.4 = (f32[24,1024]{1,0:T(8,128)}, f32[24,1024]{1,0:T(8,128)S(1)}, u32[]{:S(2)}) copy-start(f32[24,1024]{1,0:T(8,128)S(1)} %collective-permute-done.refs_1_) | copy-start | bytes 294916
  20.9 4.5 %collective-permute-start.6 = (f32[24,1024]{1,0:T(8,128)S(1)}, f32[24,1024]{1,0:T(8,128)S(1)}, u32[]{:S(2)}, u32[]{:S(2)}) collective-permute-start(f32[24,1024]{1,0:T(8,128)S(1)} %collective-permute-done.5.refs_6_), channel_id=1, source_target_pairs={{0,1},{1,0},{2,3},{3,2},{4,5},{5,4},{6,7},{7,6},{8,9},{9,8},{10,11... | collective-permute-start | bytes 294920 | tf_op jit(solution)/shard_map/ppermute | solution.py:202
  22.8 4.0 %copy-start.5 = (f32[24,1024]{1,0:T(8,128)}, f32[24,1024]{1,0:T(8,128)S(1)}, u32[]{:S(2)}) copy-start(f32[24,1024]{1,0:T(8,128)S(1)} %collective-permute-done.13.refs_14_) | copy-start | bytes 294916
  22.8 2.7 %collective-permute-start.4 = (f32[24,1024]{1,0:T(8,128)S(1)}, f32[24,1024]{1,0:T(8,128)S(1)}, u32[]{:S(2)}, u32[]{:S(2)}) collective-permute-start(f32[24,1024]{1,0:T(8,128)S(1)} %collective-permute-done.3.refs_4_), channel_id=1, source_target_pairs={{0,1},{1,0},{2,3},{3,2},{4,5},{5,4},{6,7},{7,6},{8,9},{9,8},{10,11... | collective-permute-start | bytes 294920 | tf_op jit(solution)/shard_map/ppermute | solution.py:202
  23.7 3.0 %copy-start.6 = (f32[24,1024]{1,0:T(8,128)}, f32[24,1024]{1,0:T(8,128)S(1)}, u32[]{:S(2)}) copy-start(f32[24,1024]{1,0:T(8,128)S(1)} %collective-permute-done.11.refs_12_) | copy-start | bytes 294916
  23.7 1.8 %collective-permute-start.2 = (f32[24,1024]{1,0:T(8,128)S(1)}, f32[24,1024]{1,0:T(8,128)S(1)}, u32[]{:S(2)}, u32[]{:S(2)}) collective-permute-start(f32[24,1024]{1,0:T(8,128)S(1)} %collective-permute-done.1.refs_2_), channel_id=1, source_target_pairs={{0,1},{1,0},{2,3},{3,2},{4,5},{5,4},{6,7},{7,6},{8,9},{9,8},{10,11... | collective-permute-start | bytes 294920 | tf_op jit(solution)/shard_map/ppermute | solution.py:202
  24.9 1.9 %copy-start.7 = (f32[24,1024]{1,0:T(8,128)}, f32[24,1024]{1,0:T(8,128)S(1)}, u32[]{:S(2)}) copy-start(f32[24,1024]{1,0:T(8,128)S(1)} %collective-permute-done.9.refs_10_) | copy-start | bytes 294916
  24.9 1.3 %collective-permute-start.14 = (f32[24,1024]{1,0:T(8,128)S(1)}, f32[24,1024]{1,0:T(8,128)S(1)}, u32[]{:S(2)}, u32[]{:S(2)}) collective-permute-start(f32[24,1024]{1,0:T(8,128)S(1)} %collective-permute-done.13.refs_14_), channel_id=1, source_target_pairs={{0,1},{1,0},{2,3},{3,2},{4,5},{5,4},{6,7},{7,6},{8,9},{9,8},{10,11... | collective-permute-start | bytes 294920 | tf_op jit(solution)/shard_map/ppermute | solution.py:202
  24.9 1.9 %copy-start.8 = (f32[24,1024]{1,0:T(8,128)}, f32[24,1024]{1,0:T(8,128)S(1)}, u32[]{:S(2)}) copy-start(f32[24,1024]{1,0:T(8,128)S(1)} %collective-permute-done.8.refs_9_) | copy-start | bytes 294916
  24.9 1.4 %collective-permute-start.12 = (f32[24,1024]{1,0:T(8,128)S(1)}, f32[24,1024]{1,0:T(8,128)S(1)}, u32[]{:S(2)}, u32[]{:S(2)}) collective-permute-start(f32[24,1024]{1,0:T(8,128)S(1)} %collective-permute-done.11.refs_12_), channel_id=1, source_target_pairs={{0,1},{1,0},{2,3},{3,2},{4,5},{5,4},{6,7},{7,6},{8,9},{9,8},{10,11... | collective-permute-start | bytes 294920 | tf_op jit(solution)/shard_map/ppermute | solution.py:202
  25.4 1.4 %copy-start.9 = (f32[24,1024]{1,0:T(8,128)}, f32[24,1024]{1,0:T(8,128)S(1)}, u32[]{:S(2)}) copy-start(f32[24,1024]{1,0:T(8,128)S(1)} %collective-permute-done.6.refs_7_) | copy-start | bytes 294916
  25.4 1.3 %collective-permute-start.10 = (f32[24,1024]{1,0:T(8,128)S(1)}, f32[24,1024]{1,0:T(8,128)S(1)}, u32[]{:S(2)}, u32[]{:S(2)}) collective-permute-start(f32[24,1024]{1,0:T(8,128)S(1)} %collective-permute-done.9.refs_10_), channel_id=1, source_target_pairs={{0,1},{1,0},{2,3},{3,2},{4,5},{5,4},{6,7},{7,6},{8,9},{9,8},{10,11... | collective-permute-start | bytes 294920 | tf_op jit(solution)/shard_map/ppermute | solution.py:202
  25.5 1.3 %copy-start.10 = (f32[24,1024]{1,0:T(8,128)}, f32[24,1024]{1,0:T(8,128)S(1)}, u32[]{:S(2)}) copy-start(f32[24,1024]{1,0:T(8,128)S(1)} %collective-permute-done.4.refs_5_) | copy-start | bytes 294916
  25.5 1.3 %copy-start.11 = (f32[24,1024]{1,0:T(8,128)}, f32[24,1024]{1,0:T(8,128)S(1)}, u32[]{:S(2)}) copy-start(f32[24,1024]{1,0:T(8,128)S(1)} %collective-permute-done.2.refs_3_) | copy-start | bytes 294916
  26.2 0.6 %copy-start.12 = (f32[24,1024]{1,0:T(8,128)}, f32[24,1024]{1,0:T(8,128)S(1)}, u32[]{:S(2)}) copy-start(f32[24,1024]{1,0:T(8,128)S(1)} %collective-permute-done.14.refs_15_) | copy-start | bytes 294916
  26.4 0.6 %copy-start.13 = (f32[24,1024]{1,0:T(8,128)}, f32[24,1024]{1,0:T(8,128)S(1)}, u32[]{:S(2)}) copy-start(f32[24,1024]{1,0:T(8,128)S(1)} %collective-permute-done.12.refs_13_) | copy-start | bytes 294916
  26.7 0.6 %copy-start.14 = (f32[24,1024]{1,0:T(8,128)}, f32[24,1024]{1,0:T(8,128)S(1)}, u32[]{:S(2)}) copy-start(f32[24,1024]{1,0:T(8,128)S(1)} %collective-permute-done.10.refs_11_) | copy-start | bytes 294916

commit v4 on v3

--- a/solution.py
+++ b/solution.py
@@ -124,13 +124,11 @@
     )(hidden_rows, output_grads, proj_in, proj_out, token_counts, queries)
 
 
-def times(x, n, passes):
+def times(dot, x, n, passes):
     high, mid, low = split3(x)
-    total = nt(high, high[:n]) + (nt(high, mid[:n]) + nt(mid, high[:n]))
+    total = dot(high, high[:n]) + (dot(high, mid[:n]) + dot(mid, high[:n]))
     if passes > 3:
-        total = total + nt(mid, mid[:n])
-    if passes > 4:
-        total = total + (nt(high, low[:n]) + nt(low, high[:n]))
+        total = total + (dot(mid, mid[:n]) + (dot(high, low[:n]) + dot(low, high[:n])))
     return total
 
 
@@ -147,7 +145,7 @@
         x = jnp.concatenate(
             [b[:each, k : k + n] for b in bs] + [b[each:, k : k + n] for b in bs], axis=0
         )
-        w = times(x, n, 6)
+        w = times(nt, x, n, 6)
         held[...] = w if k == 0 else held[...] + w
         squares = squares + jnp.sum(x[:n] * x[:n], axis=0, keepdims=True)
     trace = jnp.sum(squares, keepdims=True)
@@ -162,7 +160,7 @@
 
     def double(passes, level, e):
         x = held[...]
-        w = times(x, n, passes)
+        w = times(nn, x, n, passes)
         held[:n] = 4.0 * x[:n] - 2.0 * w[:n]
         held[n:] = x[n:] - w[n:] * (1.0 / (e + 2.0))
         return 2.0 * e * (e + 2.0)

time: 35.4 us -> 35 us (0.989)
  Pallas kernels: 15 us -> 14.5 us
    pallas_call x1, Pallas kernels: 7.99 us -> 7.41 us  [solve(): pl.pallas_call(functools.partial(solve_kernel, total, each, len(blocks)),...]
where the time goes in v4:
time: 35 us; the launch traced here: 34.8 us
  Pallas kernels  14.5 us (41%)
  starting transfers between devices  12.5 us (36%)
  waiting for transfers between devices  7.06 us (20%)
  local copies, waits for them, and re-layouts  0.57 us (2%)
    ppermute x15, starting transfers between devices, flip(): return lax.ppermute(x, 'dp', [(i, i ^ bits) for i in range(size)])  12.5 us
    pallas_call x1, Pallas kernels, solve(): pl.pallas_call(functools.partial(solve_kernel, total, each, len(blocks)),...  7.41 us
    pallas_call x1, Pallas kernels, project(): pl.pallas_call(functools.partial(project_kernel, size), out_shape=jax.Sha...  7.06 us
    ppermute x15, waiting for transfers between devices, flip(): return lax.ppermute(x, 'dp', [(i, i ^ bits) for i in range(size)])  7.06 us
  transfers between devices with their start and end apart: 15, of which 9 were waited for; matrix products, arithmetic and copies ran while one was open for 0% of the time, Pallas kernels for 0%

profile of v4, /device:TPU:0, one launch (start us, length us, event | category | flops | bytes accessed | tf_op | source)
XLA Modules:
  0.0 34.8 jit_solution(87927653239884382)
XLA Ops:
  0.0 7.1 %project.1.refs_0_ = f32[24,1024]{1,0:T(8,128)} custom-call(bf16[16,16,14336]{2,1,0:T(8,128)(2,1)} %hidden.1, bf16[16,16,4096]{2,1,0:T(8,128)(2,1)} %grads.1, bf16[32,14336]{1,0:T(8,128)(2,1)} %pin.1, bf16[32,4096]{1,0:T(8,128)(2,1)} %pout.1, s32[16]{0:T(128)} %counts.1, f32[8,1024]{1,0:T(8,128)} %queries.1), custom_call_target="tpu_custom_call" | custom-call | tf_op jit(solution)/shard_map/project/pallas_call | solution.py:106
  7.1 4.1 %collective-permute-start.7 = (f32[24,1024]{1,0:T(8,128)}, f32[24,1024]{1,0:T(8,128)S(1)}, u32[]{:S(2)}, u32[]{:S(2)}) collective-permute-start(f32[24,1024]{1,0:T(8,128)} %project.1.refs_0_), channel_id=1, source_target_pairs={{0,8},{1,9},{2,10},{3,11},{4,12},{5,13},{6,14},{7,15},{8,0},{9,1},... | collective-permute-start | bytes 294920 | tf_op jit(solution)/shard_map/ppermute | solution.py:200
  11.2 2.5 %collective-permute-start.5 = (f32[24,1024]{1,0:T(8,128)}, f32[24,1024]{1,0:T(8,128)S(1)}, u32[]{:S(2)}, u32[]{:S(2)}) collective-permute-start(f32[24,1024]{1,0:T(8,128)} %project.1.refs_0_), channel_id=1, source_target_pairs={{0,6},{1,7},{2,4},{3,5},{4,2},{5,3},{6,0},{7,1},{8,14},{9,15},{10,... | collective-permute-start | bytes 294920 | tf_op jit(solution)/shard_map/ppermute | solution.py:200
  13.7 0.5 %collective-permute-start.3 = (f32[24,1024]{1,0:T(8,128)}, f32[24,1024]{1,0:T(8,128)S(1)}, u32[]{:S(2)}, u32[]{:S(2)}) collective-permute-start(f32[24,1024]{1,0:T(8,128)} %project.1.refs_0_), channel_id=1, source_target_pairs={{0,4},{1,5},{2,6},{3,7},{4,0},{5,1},{6,2},{7,3},{8,12},{9,13},{10,... | collective-permute-start | bytes 294920 | tf_op jit(solution)/shard_map/ppermute | solution.py:200
  14.2 0.5 %collective-permute-start.1 = (f32[24,1024]{1,0:T(8,128)}, f32[24,1024]{1,0:T(8,128)S(1)}, u32[]{:S(2)}, u32[]{:S(2)}) collective-permute-start(f32[24,1024]{1,0:T(8,128)} %project.1.refs_0_), channel_id=1, source_target_pairs={{0,2},{1,3},{2,0},{3,1},{4,6},{5,7},{6,4},{7,5},{8,10},{9,11},{10,... | collective-permute-start | bytes 294920 | tf_op jit(solution)/shard_map/ppermute | solution.py:200
  14.6 0.0 collective-permute-start
  14.6 1.5 %collective-permute-done.7.refs_8_ = f32[24,1024]{1,0:T(8,128)S(1)} collective-permute-done((f32[24,1024]{1,0:T(8,128)}, f32[24,1024]{1,0:T(8,128)S(1)}, u32[]{:S(2)}, u32[]{:S(2)}) %collective-permute-start.7) | collective-permute-done | bytes 98336 | tf_op jit(solution)/shard_map/ppermute | solution.py:200
  16.2 2.0 %collective-permute-start.13 = (f32[24,1024]{1,0:T(8,128)S(1)}, f32[24,1024]{1,0:T(8,128)S(1)}, u32[]{:S(2)}, u32[]{:S(2)}) collective-permute-start(f32[24,1024]{1,0:T(8,128)S(1)} %collective-permute-done.7.refs_8_), channel_id=1, source_target_pairs={{0,6},{1,7},{2,4},{3,5},{4,2},{5,3},{6,0},{7,1},{8,14},{9,15},{10,... | collective-permute-start | bytes 294920 | tf_op jit(solution)/shard_map/ppermute | solution.py:200
  18.1 0.6 %collective-permute-done.5.refs_6_ = f32[24,1024]{1,0:T(8,128)S(1)} collective-permute-done((f32[24,1024]{1,0:T(8,128)}, f32[24,1024]{1,0:T(8,128)S(1)}, u32[]{:S(2)}, u32[]{:S(2)}) %collective-permute-start.5) | collective-permute-done | bytes 98336 | tf_op jit(solution)/shard_map/ppermute | solution.py:200
  18.7 1.3 %collective-permute-start.11 = (f32[24,1024]{1,0:T(8,128)S(1)}, f32[24,1024]{1,0:T(8,128)S(1)}, u32[]{:S(2)}, u32[]{:S(2)}) collective-permute-start(f32[24,1024]{1,0:T(8,128)S(1)} %collective-permute-done.7.refs_8_), channel_id=1, source_target_pairs={{0,4},{1,5},{2,6},{3,7},{4,0},{5,1},{6,2},{7,3},{8,12},{9,13},{10,... | collective-permute-start | bytes 294920 | tf_op jit(solution)/shard_map/ppermute | solution.py:200
  20.0 0.3 collective-permute-done.3.refs_4_
  20.3 0.6 %collective-permute-start.9 = (f32[24,1024]{1,0:T(8,128)S(1)}, f32[24,1024]{1,0:T(8,128)S(1)}, u32[]{:S(2)}, u32[]{:S(2)}) collective-permute-start(f32[24,1024]{1,0:T(8,128)S(1)} %collective-permute-done.7.refs_8_), channel_id=1, source_target_pairs={{0,2},{1,3},{2,0},{3,1},{4,6},{5,7},{6,4},{7,5},{8,10},{9,11},{10,... | collective-permute-start | bytes 294920 | tf_op jit(solution)/shard_map/ppermute | solution.py:200
  20.9 0.0 collective-permute-done.1.refs_2_
  20.9 0.0 collective-permute-start.8
  20.9 0.0 collective-permute-done.refs_1_
  20.9 0.5 %collective-permute-start.6 = (f32[24,1024]{1,0:T(8,128)S(1)}, f32[24,1024]{1,0:T(8,128)S(1)}, u32[]{:S(2)}, u32[]{:S(2)}) collective-permute-start(f32[24,1024]{1,0:T(8,128)S(1)} %collective-permute-done.5.refs_6_), channel_id=1, source_target_pairs={{0,1},{1,0},{2,3},{3,2},{4,5},{5,4},{6,7},{7,6},{8,9},{9,8},{10,11... | collective-permute-start | bytes 294920 | tf_op jit(solution)/shard_map/ppermute | solution.py:200
  21.4 1.4 %collective-permute-done.13.refs_14_ = f32[24,1024]{1,0:T(8,128)S(1)} collective-permute-done((f32[24,1024]{1,0:T(8,128)S(1)}, f32[24,1024]{1,0:T(8,128)S(1)}, u32[]{:S(2)}, u32[]{:S(2)}) %collective-permute-start.13) | collective-permute-done | bytes 98336 | tf_op jit(solution)/shard_map/ppermute | solution.py:200
  22.8 0.0 collective-permute-start.4
  22.8 1.0 %collective-permute-done.11.refs_12_ = f32[24,1024]{1,0:T(8,128)S(1)} collective-permute-done((f32[24,1024]{1,0:T(8,128)S(1)}, f32[24,1024]{1,0:T(8,128)S(1)}, u32[]{:S(2)}, u32[]{:S(2)}) %collective-permute-start.11) | collective-permute-done | bytes 98336 | tf_op jit(solution)/shard_map/ppermute | solution.py:200
  23.7 0.0 collective-permute-start.2
  23.7 1.2 %collective-permute-done.9.refs_10_ = f32[24,1024]{1,0:T(8,128)S(1)} collective-permute-done((f32[24,1024]{1,0:T(8,128)S(1)}, f32[24,1024]{1,0:T(8,128)S(1)}, u32[]{:S(2)}, u32[]{:S(2)}) %collective-permute-start.9) | collective-permute-done | bytes 98336 | tf_op jit(solution)/shard_map/ppermute | solution.py:200
  24.9 0.0 collective-permute-start.14
  24.9 0.0 collective-permute-done.8.refs_9_
  24.9 0.5 %collective-permute-start.12 = (f32[24,1024]{1,0:T(8,128)S(1)}, f32[24,1024]{1,0:T(8,128)S(1)}, u32[]{:S(2)}, u32[]{:S(2)}) collective-permute-start(f32[24,1024]{1,0:T(8,128)S(1)} %collective-permute-done.11.refs_12_), channel_id=1, source_target_pairs={{0,1},{1,0},{2,3},{3,2},{4,5},{5,4},{6,7},{7,6},{8,9},{9,8},{10,11... | collective-permute-start | bytes 294920 | tf_op jit(solution)/shard_map/ppermute | solution.py:200
  25.4 0.1 collective-permute-start.10
  25.5 0.7 %collective-permute-done.14.refs_15_ = f32[24,1024]{1,0:T(8,128)S(1)} collective-permute-done((f32[24,1024]{1,0:T(8,128)S(1)}, f32[24,1024]{1,0:T(8,128)S(1)}, u32[]{:S(2)}, u32[]{:S(2)}) %collective-permute-start.14) | collective-permute-done | bytes 98336 | tf_op jit(solution)/shard_map/ppermute | solution.py:200
  26.2 0.2 collective-permute-done.12.refs_13_
  26.4 0.4 %collective-permute-done.10.refs_11_ = f32[24,1024]{1,0:T(8,128)S(1)} collective-permute-done((f32[24,1024]{1,0:T(8,128)S(1)}, f32[24,1024]{1,0:T(8,128)S(1)}, u32[]{:S(2)}, u32[]{:S(2)}) %collective-permute-start.10) | collective-permute-done | bytes 98336 | tf_op jit(solution)/shard_map/ppermute | solution.py:200
  26.8 0.0 copy-done.12
  26.8 0.2 copy-done.13
  27.0 0.4 %copy-done.14 = f32[24,1024]{1,0:T(8,128)} copy-done((f32[24,1024]{1,0:T(8,128)}, f32[24,1024]{1,0:T(8,128)S(1)}, u32[]{:S(2)}) %copy-start.14) | copy-done | bytes 98328
  27.4 7.4 %solve.1 = f32[16,128]{1,0:T(8,128)} custom-call(f32[24,1024]{1,0:T(8,128)} %project.1.refs_0_, f32[24,1024]{1,0:T(8,128)} %copy-done.4, f32[24,1024]{1,0:T(8,128)} %copy-done.3, f32[24,1024]{1,0:T(8,128)} %copy-done.11, f32[24,1024]{1,0:T(8,128)} %copy-done.2, f32[24,1024]{1,0:T(8,128)} %copy-done.10, f32[24,1024]{1,0:T(8,128)} %copy-done.1, ...), custom_call_target="tpu_custom_call" | custom-call | tf_op jit(solution)/shard_map/solve/pallas_call | solution.py:188
  (30 shorter events, 0.1 us)
Async XLA Ops:
  7.1 9.1 %collective-permute-start.7 = (f32[24,1024]{1,0:T(8,128)}, f32[24,1024]{1,0:T(8,128)S(1)}, u32[]{:S(2)}, u32[]{:S(2)}) collective-permute-start(f32[24,1024]{1,0:T(8,128)} %project.1.refs_0_), channel_id=1, source_target_pairs={{0,8},{1,9},{2,10},{3,11},{4,12},{5,13},{6,14},{7,15},{8,0},{9,1},... | collective-permute-start | bytes 294920 | tf_op jit(solution)/shard_map/ppermute | solution.py:200
  11.2 7.6 %collective-permute-start.5 = (f32[24,1024]{1,0:T(8,128)}, f32[24,1024]{1,0:T(8,128)S(1)}, u32[]{:S(2)}, u32[]{:S(2)}) collective-permute-start(f32[24,1024]{1,0:T(8,128)} %project.1.refs_0_), channel_id=1, source_target_pairs={{0,6},{1,7},{2,4},{3,5},{4,2},{5,3},{6,0},{7,1},{8,14},{9,15},{10,... | collective-permute-start | bytes 294920 | tf_op jit(solution)/shard_map/ppermute | solution.py:200
  13.7 6.6 %collective-permute-start.3 = (f32[24,1024]{1,0:T(8,128)}, f32[24,1024]{1,0:T(8,128)S(1)}, u32[]{:S(2)}, u32[]{:S(2)}) collective-permute-start(f32[24,1024]{1,0:T(8,128)} %project.1.refs_0_), channel_id=1, source_target_pairs={{0,4},{1,5},{2,6},{3,7},{4,0},{5,1},{6,2},{7,3},{8,12},{9,13},{10,... | collective-permute-start | bytes 294920 | tf_op jit(solution)/shard_map/ppermute | solution.py:200
  14.2 6.7 %collective-permute-start.1 = (f32[24,1024]{1,0:T(8,128)}, f32[24,1024]{1,0:T(8,128)S(1)}, u32[]{:S(2)}, u32[]{:S(2)}) collective-permute-start(f32[24,1024]{1,0:T(8,128)} %project.1.refs_0_), channel_id=1, source_target_pairs={{0,2},{1,3},{2,0},{3,1},{4,6},{5,7},{6,4},{7,5},{8,10},{9,11},{10,... | collective-permute-start | bytes 294920 | tf_op jit(solution)/shard_map/ppermute | solution.py:200
  14.6 6.2 %collective-permute-start = (f32[24,1024]{1,0:T(8,128)}, f32[24,1024]{1,0:T(8,128)S(1)}, u32[]{:S(2)}, u32[]{:S(2)}) collective-permute-start(f32[24,1024]{1,0:T(8,128)} %project.1.refs_0_), channel_id=1, source_target_pairs={{0,1},{1,0},{2,3},{3,2},{4,5},{5,4},{6,7},{7,6},{8,9},{9,8},{10,11... | collective-permute-start | bytes 294920 | tf_op jit(solution)/shard_map/ppermute | solution.py:200
  16.2 10.6 %copy-start = (f32[24,1024]{1,0:T(8,128)}, f32[24,1024]{1,0:T(8,128)S(1)}, u32[]{:S(2)}) copy-start(f32[24,1024]{1,0:T(8,128)S(1)} %collective-permute-done.7.refs_8_) | copy-start | bytes 294916
  16.2 6.6 %collective-permute-start.13 = (f32[24,1024]{1,0:T(8,128)S(1)}, f32[24,1024]{1,0:T(8,128)S(1)}, u32[]{:S(2)}, u32[]{:S(2)}) collective-permute-start(f32[24,1024]{1,0:T(8,128)S(1)} %collective-permute-done.7.refs_8_), channel_id=1, source_target_pairs={{0,6},{1,7},{2,4},{3,5},{4,2},{5,3},{6,0},{7,1},{8,14},{9,15},{10,... | collective-permute-start | bytes 294920 | tf_op jit(solution)/shard_map/ppermute | solution.py:200
  18.7 8.0 %copy-start.1 = (f32[24,1024]{1,0:T(8,128)}, f32[24,1024]{1,0:T(8,128)S(1)}, u32[]{:S(2)}) copy-start(f32[24,1024]{1,0:T(8,128)S(1)} %collective-permute-done.5.refs_6_) | copy-start | bytes 294916
  18.7 5.0 %collective-permute-start.11 = (f32[24,1024]{1,0:T(8,128)S(1)}, f32[24,1024]{1,0:T(8,128)S(1)}, u32[]{:S(2)}, u32[]{:S(2)}) collective-permute-start(f32[24,1024]{1,0:T(8,128)S(1)} %collective-permute-done.7.refs_8_), channel_id=1, source_target_pairs={{0,4},{1,5},{2,6},{3,7},{4,0},{5,1},{6,2},{7,3},{8,12},{9,13},{10,... | collective-permute-start | bytes 294920 | tf_op jit(solution)/shard_map/ppermute | solution.py:200
  20.3 6.5 %copy-start.2 = (f32[24,1024]{1,0:T(8,128)}, f32[24,1024]{1,0:T(8,128)S(1)}, u32[]{:S(2)}) copy-start(f32[24,1024]{1,0:T(8,128)S(1)} %collective-permute-done.3.refs_4_) | copy-start | bytes 294916
  20.3 4.6 %collective-permute-start.9 = (f32[24,1024]{1,0:T(8,128)S(1)}, f32[24,1024]{1,0:T(8,128)S(1)}, u32[]{:S(2)}, u32[]{:S(2)}) collective-permute-start(f32[24,1024]{1,0:T(8,128)S(1)} %collective-permute-done.7.refs_8_), channel_id=1, source_target_pairs={{0,2},{1,3},{2,0},{3,1},{4,6},{5,7},{6,4},{7,5},{8,10},{9,11},{10,... | collective-permute-start | bytes 294920 | tf_op jit(solution)/shard_map/ppermute | solution.py:200
  20.9 5.9 %copy-start.3 = (f32[24,1024]{1,0:T(8,128)}, f32[24,1024]{1,0:T(8,128)S(1)}, u32[]{:S(2)}) copy-start(f32[24,1024]{1,0:T(8,128)S(1)} %collective-permute-done.1.refs_2_) | copy-start | bytes 294916
  20.9 4.0 %collective-permute-start.8 = (f32[24,1024]{1,0:T(8,128)S(1)}, f32[24,1024]{1,0:T(8,128)S(1)}, u32[]{:S(2)}, u32[]{:S(2)}) collective-permute-start(f32[24,1024]{1,0:T(8,128)S(1)} %collective-permute-done.7.refs_8_), channel_id=1, source_target_pairs={{0,1},{1,0},{2,3},{3,2},{4,5},{5,4},{6,7},{7,6},{8,9},{9,8},{10,11... | collective-permute-start | bytes 294920 | tf_op jit(solution)/shard_map/ppermute | solution.py:200
  20.9 5.9 %copy-start.4 = (f32[24,1024]{1,0:T(8,128)}, f32[24,1024]{1,0:T(8,128)S(1)}, u32[]{:S(2)}) copy-start(f32[24,1024]{1,0:T(8,128)S(1)} %collective-permute-done.refs_1_) | copy-start | bytes 294916
  20.9 4.5 %collective-permute-start.6 = (f32[24,1024]{1,0:T(8,128)S(1)}, f32[24,1024]{1,0:T(8,128)S(1)}, u32[]{:S(2)}, u32[]{:S(2)}) collective-permute-start(f32[24,1024]{1,0:T(8,128)S(1)} %collective-permute-done.5.refs_6_), channel_id=1, source_target_pairs={{0,1},{1,0},{2,3},{3,2},{4,5},{5,4},{6,7},{7,6},{8,9},{9,8},{10,11... | collective-permute-start | bytes 294920 | tf_op jit(solution)/shard_map/ppermute | solution.py:200
  22.8 4.0 %copy-start.5 = (f32[24,1024]{1,0:T(8,128)}, f32[24,1024]{1,0:T(8,128)S(1)}, u32[]{:S(2)}) copy-start(f32[24,1024]{1,0:T(8,128)S(1)} %collective-permute-done.13.refs_14_) | copy-start | bytes 294916
  22.8 2.7 %collective-permute-start.4 = (f32[24,1024]{1,0:T(8,128)S(1)}, f32[24,1024]{1,0:T(8,128)S(1)}, u32[]{:S(2)}, u32[]{:S(2)}) collective-permute-start(f32[24,1024]{1,0:T(8,128)S(1)} %collective-permute-done.3.refs_4_), channel_id=1, source_target_pairs={{0,1},{1,0},{2,3},{3,2},{4,5},{5,4},{6,7},{7,6},{8,9},{9,8},{10,11... | collective-permute-start | bytes 294920 | tf_op jit(solution)/shard_map/ppermute | solution.py:200
  23.7 3.0 %copy-start.6 = (f32[24,1024]{1,0:T(8,128)}, f32[24,1024]{1,0:T(8,128)S(1)}, u32[]{:S(2)}) copy-start(f32[24,1024]{1,0:T(8,128)S(1)} %collective-permute-done.11.refs_12_) | copy-start | bytes 294916
  23.7 1.8 %collective-permute-start.2 = (f32[24,1024]{1,0:T(8,128)S(1)}, f32[24,1024]{1,0:T(8,128)S(1)}, u32[]{:S(2)}, u32[]{:S(2)}) collective-permute-start(f32[24,1024]{1,0:T(8,128)S(1)} %collective-permute-done.1.refs_2_), channel_id=1, source_target_pairs={{0,1},{1,0},{2,3},{3,2},{4,5},{5,4},{6,7},{7,6},{8,9},{9,8},{10,11... | collective-permute-start | bytes 294920 | tf_op jit(solution)/shard_map/ppermute | solution.py:200
  24.9 1.9 %copy-start.7 = (f32[24,1024]{1,0:T(8,128)}, f32[24,1024]{1,0:T(8,128)S(1)}, u32[]{:S(2)}) copy-start(f32[24,1024]{1,0:T(8,128)S(1)} %collective-permute-done.9.refs_10_) | copy-start | bytes 294916
  24.9 1.3 %collective-permute-start.14 = (f32[24,1024]{1,0:T(8,128)S(1)}, f32[24,1024]{1,0:T(8,128)S(1)}, u32[]{:S(2)}, u32[]{:S(2)}) collective-permute-start(f32[24,1024]{1,0:T(8,128)S(1)} %collective-permute-done.13.refs_14_), channel_id=1, source_target_pairs={{0,1},{1,0},{2,3},{3,2},{4,5},{5,4},{6,7},{7,6},{8,9},{9,8},{10,11... | collective-permute-start | bytes 294920 | tf_op jit(solution)/shard_map/ppermute | solution.py:200
  24.9 1.9 %copy-start.8 = (f32[24,1024]{1,0:T(8,128)}, f32[24,1024]{1,0:T(8,128)S(1)}, u32[]{:S(2)}) copy-start(f32[24,1024]{1,0:T(8,128)S(1)} %collective-permute-done.8.refs_9_) | copy-start | bytes 294916
  24.9 1.4 %collective-permute-start.12 = (f32[24,1024]{1,0:T(8,128)S(1)}, f32[24,1024]{1,0:T(8,128)S(1)}, u32[]{:S(2)}, u32[]{:S(2)}) collective-permute-start(f32[24,1024]{1,0:T(8,128)S(1)} %collective-permute-done.11.refs_12_), channel_id=1, source_target_pairs={{0,1},{1,0},{2,3},{3,2},{4,5},{5,4},{6,7},{7,6},{8,9},{9,8},{10,11... | collective-permute-start | bytes 294920 | tf_op jit(solution)/shard_map/ppermute | solution.py:200
  25.4 1.4 %copy-start.9 = (f32[24,1024]{1,0:T(8,128)}, f32[24,1024]{1,0:T(8,128)S(1)}, u32[]{:S(2)}) copy-start(f32[24,1024]{1,0:T(8,128)S(1)} %collective-permute-done.6.refs_7_) | copy-start | bytes 294916
  25.4 1.3 %collective-permute-start.10 = (f32[24,1024]{1,0:T(8,128)S(1)}, f32[24,1024]{1,0:T(8,128)S(1)}, u32[]{:S(2)}, u32[]{:S(2)}) collective-permute-start(f32[24,1024]{1,0:T(8,128)S(1)} %collective-permute-done.9.refs_10_), channel_id=1, source_target_pairs={{0,1},{1,0},{2,3},{3,2},{4,5},{5,4},{6,7},{7,6},{8,9},{9,8},{10,11... | collective-permute-start | bytes 294920 | tf_op jit(solution)/shard_map/ppermute | solution.py:200
  25.5 1.3 %copy-start.10 = (f32[24,1024]{1,0:T(8,128)}, f32[24,1024]{1,0:T(8,128)S(1)}, u32[]{:S(2)}) copy-start(f32[24,1024]{1,0:T(8,128)S(1)} %collective-permute-done.4.refs_5_) | copy-start | bytes 294916
  25.5 1.3 %copy-start.11 = (f32[24,1024]{1,0:T(8,128)}, f32[24,1024]{1,0:T(8,128)S(1)}, u32[]{:S(2)}) copy-start(f32[24,1024]{1,0:T(8,128)S(1)} %collective-permute-done.2.refs_3_) | copy-start | bytes 294916
  26.2 0.6 %copy-start.12 = (f32[24,1024]{1,0:T(8,128)}, f32[24,1024]{1,0:T(8,128)S(1)}, u32[]{:S(2)}) copy-start(f32[24,1024]{1,0:T(8,128)S(1)} %collective-permute-done.14.refs_15_) | copy-start | bytes 294916
  26.4 0.6 %copy-start.13 = (f32[24,1024]{1,0:T(8,128)}, f32[24,1024]{1,0:T(8,128)S(1)}, u32[]{:S(2)}) copy-start(f32[24,1024]{1,0:T(8,128)S(1)} %collective-permute-done.12.refs_13_) | copy-start | bytes 294916
  26.7 0.6 %copy-start.14 = (f32[24,1024]{1,0:T(8,128)}, f32[24,1024]{1,0:T(8,128)S(1)}, u32[]{:S(2)}) copy-start(f32[24,1024]{1,0:T(8,128)S(1)} %collective-permute-done.10.refs_11_) | copy-start | bytes 294916

commit v5 on v4

--- a/solution.py
+++ b/solution.py
@@ -11,7 +11,8 @@
 f32 = jnp.float32
 bf16 = jnp.bfloat16
 levels = 9
-vmem_bytes = 60 * 2**20
+project_vmem = 60 * 2**20
+solve_vmem = 16 * 2**20
 
 
 def split3(x):
@@ -31,7 +32,7 @@
 
 
 def project_kernel(
-    size, hidden, grads, pin, pout, counts, queries, out, hbuf, gbuf, pibuf, pobuf, left, sems
+    size, hidden, grads, pin, pout, live_in, queries, out, hbuf, gbuf, pibuf, pobuf, left, counts, sems
 ):
     pieces, examples, seq, _ = hbuf.shape
     model = gbuf.shape[2]
@@ -43,6 +44,11 @@
         pltpu.make_async_copy(grads, gbuf, sems.at[1]),
     ]
 
+    late = [
+        pltpu.make_async_copy(live_in, counts, sems.at[2 + 2 * pieces]),
+        pltpu.make_async_copy(queries, out.at[examples:], sems.at[3 + 2 * pieces]),
+    ]
+
     def piece(i):
         across = pl.ds(pl.multiple_of(i * size, 128), size)
         return (
@@ -57,6 +63,8 @@
     for i in range(pieces):
         for copy in piece(i):
             copy.start()
+    for copy in late:
+        copy.start()
     for copy in first:
         copy.wait()
     left[...] = jnp.zeros((rows, rank), f32)
@@ -69,6 +77,8 @@
         return carry
 
     lax.fori_loop(0, pieces, work, 0)
+    for copy in late:
+        copy.wait()
     example = lax.broadcasted_iota(jnp.int32, (examples, 1), 0)
     live = jnp.zeros((examples, 1), jnp.int32)
     for e in range(examples):
@@ -93,7 +103,6 @@
         )
         total = jnp.sum(product.reshape(seq, examples, step), axis=0)
         out[:examples, c : c + step] = total / over
-    out[examples:] = queries[...]
 
 
 def project(hidden_rows, output_grads, proj_in, proj_out, token_counts, queries):
@@ -106,10 +115,7 @@
     return pl.pallas_call(
         functools.partial(project_kernel, size),
         out_shape=jax.ShapeDtypeStruct((examples + queries.shape[0], rank * rank), f32),
-        in_specs=[anywhere] * 4 + [
-            pl.BlockSpec(memory_space=pltpu.SMEM),
-            pl.BlockSpec(memory_space=pltpu.VMEM),
-        ],
+        in_specs=[anywhere] * 6,
         out_specs=pl.BlockSpec(memory_space=pltpu.VMEM),
         scratch_shapes=[
             pltpu.VMEM((pieces, examples, seq, size), bf16),
@@ -117,9 +123,10 @@
             pltpu.VMEM((pieces, rank, size), bf16),
             pltpu.VMEM(proj_out.shape, bf16),
             pltpu.VMEM((examples * seq, rank), f32),
-            pltpu.SemaphoreType.DMA((2 + 2 * pieces,)),
+            pltpu.SMEM(token_counts.shape, jnp.int32),
+            pltpu.SemaphoreType.DMA((4 + 2 * pieces,)),
         ],
-        compiler_params=pltpu.CompilerParams(vmem_limit_bytes=vmem_bytes),
+        compiler_params=pltpu.CompilerParams(vmem_limit_bytes=project_vmem),
         name="project",
     )(hidden_rows, output_grads, proj_in, proj_out, token_counts, queries)
 
@@ -191,7 +198,7 @@
         in_specs=[pl.BlockSpec(memory_space=pltpu.VMEM)] * (len(blocks) + 1),
         out_specs=pl.BlockSpec(memory_space=pltpu.VMEM),
         scratch_shapes=[pltpu.VMEM((n + asked, n), f32)],
-        compiler_params=pltpu.CompilerParams(vmem_limit_bytes=vmem_bytes),
+        compiler_params=pltpu.CompilerParams(vmem_limit_bytes=solve_vmem),
         name="solve",
     )(*blocks, slots.reshape(1, asked))
 
@@ -208,6 +215,7 @@
         got[8 + k] = flip(got[8], k, size)
     for k in (0, 8, 2, 4, 6, 10, 12, 14):
         got[k + 1] = flip(got[k], 1, size)
+    got[0] = flip(got[1], 1, size)
     return [got[k] for k in range(size)]
 
 

time: 35 us -> 32.3 us (0.923)
  Pallas kernels: 14.5 us -> 12.3 us
  local copies, waits for them, and re-layouts: 0.57 us -> 0.01 us
  starting transfers between devices: 12.5 us -> 12.9 us
    pallas_call x1, Pallas kernels: 7.41 us -> 5.98 us  [solve(): pl.pallas_call(functools.partial(solve_kernel, total, each, len(blocks)),...]
    pallas_call x1, Pallas kernels: 7.06 us -> 6.36 us  [project(): pl.pallas_call(functools.partial(project_kernel, size), out_shape=jax.Sha...]
    unnamed x30 -> x2, local copies, waits for them, and re-layouts: 0.57 us -> 0.01 us
    ppermute x15 -> x16, starting transfers between devices: 12.5 us -> 12.9 us  [flip(): return lax.ppermute(x, 'dp', [(i, i ^ bits) for i in range(size)])]
    ppermute x15 -> x16, waiting for transfers between devices: 7.06 us -> 6.9 us  [flip(): return lax.ppermute(x, 'dp', [(i, i ^ bits) for i in range(size)])]
  transfers between devices with their start and end apart: 15 -> 16, of which waited for: 9 -> 10; matrix products, arithmetic and copies ran while one was open for 0% -> 0% of each run, Pallas kernels for 0% -> 0%
where the time goes in v5:
time: 32.3 us; the launch traced here: 32.2 us
  starting transfers between devices  12.9 us (40%)
  Pallas kernels  12.3 us (38%)
  waiting for transfers between devices  6.9 us (21%)
    ppermute x16, starting transfers between devices, flip(): return lax.ppermute(x, 'dp', [(i, i ^ bits) for i in range(size)])  12.9 us
    ppermute x16, waiting for transfers between devices, flip(): return lax.ppermute(x, 'dp', [(i, i ^ bits) for i in range(size)])  6.9 us
    pallas_call x1, Pallas kernels, project(): pl.pallas_call(functools.partial(project_kernel, size), out_shape=jax.Sha...  6.36 us
    pallas_call x1, Pallas kernels, solve(): pl.pallas_call(functools.partial(solve_kernel, total, each, len(blocks)),...  5.98 us
  transfers between devices with their start and end apart: 16, of which 10 were waited for; matrix products, arithmetic and copies ran while one was open for 0% of the time, Pallas kernels for 0%

profile of v5, /device:TPU:0, one launch (start us, length us, event | category | flops | bytes accessed | tf_op | source)
XLA Modules:
  0.0 32.2 jit_solution(7433798519140365536)
XLA Ops:
  0.0 6.4 %project.1 = f32[24,1024]{1,0:T(8,128)} custom-call(bf16[16,16,14336]{2,1,0:T(8,128)(2,1)} %hidden.1, bf16[16,16,4096]{2,1,0:T(8,128)(2,1)} %grads.1, bf16[32,14336]{1,0:T(8,128)(2,1)} %pin.1, bf16[32,4096]{1,0:T(8,128)(2,1)} %pout.1, s32[16]{0:T(128)} %live_in.1, f32[8,1024]{1,0:T(8,128)} %queries.1), custom_call_target="tpu_custom_call" | custom-call | tf_op jit(solution)/shard_map/project/pallas_call | solution.py:115
  6.4 4.1 %collective-permute-start.8 = (f32[24,1024]{1,0:T(8,128)}, f32[24,1024]{1,0:T(8,128)S(1)}, u32[]{:S(2)}, u32[]{:S(2)}) collective-permute-start(f32[24,1024]{1,0:T(8,128)} %project.1), channel_id=1, source_target_pairs={{0,8},{1,9},{2,10},{3,11},{4,12},{5,13},{6,14},{7,15},{8,0},{9,1},... | collective-permute-start | bytes 294920 | tf_op jit(solution)/shard_map/ppermute | solution.py:207
  10.5 2.5 %collective-permute-start.6 = (f32[24,1024]{1,0:T(8,128)}, f32[24,1024]{1,0:T(8,128)S(1)}, u32[]{:S(2)}, u32[]{:S(2)}) collective-permute-start(f32[24,1024]{1,0:T(8,128)} %project.1), channel_id=1, source_target_pairs={{0,6},{1,7},{2,4},{3,5},{4,2},{5,3},{6,0},{7,1},{8,14},{9,15},{10,... | collective-permute-start | bytes 294920 | tf_op jit(solution)/shard_map/ppermute | solution.py:207
  13.0 0.4 %collective-permute-start.4 = (f32[24,1024]{1,0:T(8,128)}, f32[24,1024]{1,0:T(8,128)S(1)}, u32[]{:S(2)}, u32[]{:S(2)}) collective-permute-start(f32[24,1024]{1,0:T(8,128)} %project.1), channel_id=1, source_target_pairs={{0,4},{1,5},{2,6},{3,7},{4,0},{5,1},{6,2},{7,3},{8,12},{9,13},{10,... | collective-permute-start | bytes 294920 | tf_op jit(solution)/shard_map/ppermute | solution.py:207
  13.4 0.5 %collective-permute-start.2 = (f32[24,1024]{1,0:T(8,128)}, f32[24,1024]{1,0:T(8,128)S(1)}, u32[]{:S(2)}, u32[]{:S(2)}) collective-permute-start(f32[24,1024]{1,0:T(8,128)} %project.1), channel_id=1, source_target_pairs={{0,2},{1,3},{2,0},{3,1},{4,6},{5,7},{6,4},{7,5},{8,10},{9,11},{10,... | collective-permute-start | bytes 294920 | tf_op jit(solution)/shard_map/ppermute | solution.py:207
  14.0 0.0 collective-permute-start
  14.0 1.5 %collective-permute-done.8.refs_8_ = f32[24,1024]{1,0:T(8,128)S(1)} collective-permute-done((f32[24,1024]{1,0:T(8,128)}, f32[24,1024]{1,0:T(8,128)S(1)}, u32[]{:S(2)}, u32[]{:S(2)}) %collective-permute-start.8) | collective-permute-done | bytes 98336 | tf_op jit(solution)/shard_map/ppermute | solution.py:207
  15.5 1.9 %collective-permute-start.14 = (f32[24,1024]{1,0:T(8,128)S(1)}, f32[24,1024]{1,0:T(8,128)S(1)}, u32[]{:S(2)}, u32[]{:S(2)}) collective-permute-start(f32[24,1024]{1,0:T(8,128)S(1)} %collective-permute-done.8.refs_8_), channel_id=1, source_target_pairs={{0,6},{1,7},{2,4},{3,5},{4,2},{5,3},{6,0},{7,1},{8,14},{9,15},{10,... | collective-permute-start | bytes 294920 | tf_op jit(solution)/shard_map/ppermute | solution.py:207
  17.4 0.6 %collective-permute-done.6.refs_6_ = f32[24,1024]{1,0:T(8,128)S(1)} collective-permute-done((f32[24,1024]{1,0:T(8,128)}, f32[24,1024]{1,0:T(8,128)S(1)}, u32[]{:S(2)}, u32[]{:S(2)}) %collective-permute-start.6) | collective-permute-done | bytes 98336 | tf_op jit(solution)/shard_map/ppermute | solution.py:207
  18.0 1.3 %collective-permute-start.12 = (f32[24,1024]{1,0:T(8,128)S(1)}, f32[24,1024]{1,0:T(8,128)S(1)}, u32[]{:S(2)}, u32[]{:S(2)}) collective-permute-start(f32[24,1024]{1,0:T(8,128)S(1)} %collective-permute-done.8.refs_8_), channel_id=1, source_target_pairs={{0,4},{1,5},{2,6},{3,7},{4,0},{5,1},{6,2},{7,3},{8,12},{9,13},{10,... | collective-permute-start | bytes 294920 | tf_op jit(solution)/shard_map/ppermute | solution.py:207
  19.3 0.3 collective-permute-done.4.refs_4_
  19.6 0.6 %collective-permute-start.10 = (f32[24,1024]{1,0:T(8,128)S(1)}, f32[24,1024]{1,0:T(8,128)S(1)}, u32[]{:S(2)}, u32[]{:S(2)}) collective-permute-start(f32[24,1024]{1,0:T(8,128)S(1)} %collective-permute-done.8.refs_8_), channel_id=1, source_target_pairs={{0,2},{1,3},{2,0},{3,1},{4,6},{5,7},{6,4},{7,5},{8,10},{9,11},{10,... | collective-permute-start | bytes 294920 | tf_op jit(solution)/shard_map/ppermute | solution.py:207
  20.2 0.0 collective-permute-done.2.refs_2_
  20.2 0.0 collective-permute-start.9
  20.2 0.0 collective-permute-done.refs_1_
  20.2 0.5 %collective-permute-start.7 = (f32[24,1024]{1,0:T(8,128)S(1)}, f32[24,1024]{1,0:T(8,128)S(1)}, u32[]{:S(2)}, u32[]{:S(2)}) collective-permute-start(f32[24,1024]{1,0:T(8,128)S(1)} %collective-permute-done.6.refs_6_), channel_id=1, source_target_pairs={{0,1},{1,0},{2,3},{3,2},{4,5},{5,4},{6,7},{7,6},{8,9},{9,8},{10,11... | collective-permute-start | bytes 294920 | tf_op jit(solution)/shard_map/ppermute | solution.py:207
  20.7 1.4 %collective-permute-done.14.refs_14_ = f32[24,1024]{1,0:T(8,128)S(1)} collective-permute-done((f32[24,1024]{1,0:T(8,128)S(1)}, f32[24,1024]{1,0:T(8,128)S(1)}, u32[]{:S(2)}, u32[]{:S(2)}) %collective-permute-start.14) | collective-permute-done | bytes 98336 | tf_op jit(solution)/shard_map/ppermute | solution.py:207
  22.1 0.0 collective-permute-start.5
  22.1 0.9 %collective-permute-done.12.refs_12_ = f32[24,1024]{1,0:T(8,128)S(1)} collective-permute-done((f32[24,1024]{1,0:T(8,128)S(1)}, f32[24,1024]{1,0:T(8,128)S(1)}, u32[]{:S(2)}, u32[]{:S(2)}) %collective-permute-start.12) | collective-permute-done | bytes 98336 | tf_op jit(solution)/shard_map/ppermute | solution.py:207
  23.1 0.0 collective-permute-start.3
  23.1 1.2 %collective-permute-done.10.refs_10_ = f32[24,1024]{1,0:T(8,128)S(1)} collective-permute-done((f32[24,1024]{1,0:T(8,128)S(1)}, f32[24,1024]{1,0:T(8,128)S(1)}, u32[]{:S(2)}, u32[]{:S(2)}) %collective-permute-start.10) | collective-permute-done | bytes 98336 | tf_op jit(solution)/shard_map/ppermute | solution.py:207
  24.2 0.0 collective-permute-start.1
  24.2 0.0 collective-permute-done.9.refs_9_
  24.2 0.5 %collective-permute-start.15 = (f32[24,1024]{1,0:T(8,128)S(1)}, f32[24,1024]{1,0:T(8,128)S(1)}, u32[]{:S(2)}, u32[]{:S(2)}) collective-permute-start(f32[24,1024]{1,0:T(8,128)S(1)} %collective-permute-done.14.refs_14_), channel_id=1, source_target_pairs={{0,1},{1,0},{2,3},{3,2},{4,5},{5,4},{6,7},{7,6},{8,9},{9,8},{10,11... | collective-permute-start | bytes 294920 | tf_op jit(solution)/shard_map/ppermute | solution.py:207
  24.7 0.0 collective-permute-done.7.refs_7_
  24.7 0.1 collective-permute-start.13
  24.8 0.4 %collective-permute-start.11 = (f32[24,1024]{1,0:T(8,128)S(1)}, f32[24,1024]{1,0:T(8,128)S(1)}, u32[]{:S(2)}, u32[]{:S(2)}) collective-permute-start(f32[24,1024]{1,0:T(8,128)S(1)} %collective-permute-done.10.refs_10_), channel_id=1, source_target_pairs={{0,1},{1,0},{2,3},{3,2},{4,5},{5,4},{6,7},{7,6},{8,9},{9,8},{10,11... | collective-permute-start | bytes 294920 | tf_op jit(solution)/shard_map/ppermute | solution.py:207
  25.3 0.3 collective-permute-done.1.refs_0_
  25.5 0.2 collective-permute-done.15.refs_15_
  25.7 0.4 %collective-permute-done.13.refs_13_ = f32[24,1024]{1,0:T(8,128)S(1)} collective-permute-done((f32[24,1024]{1,0:T(8,128)S(1)}, f32[24,1024]{1,0:T(8,128)S(1)}, u32[]{:S(2)}, u32[]{:S(2)}) %collective-permute-start.13) | collective-permute-done | bytes 98336 | tf_op jit(solution)/shard_map/ppermute | solution.py:207
  26.0 0.2 collective-permute-done.11.refs_11_
  26.2 6.0 %solve.1 = f32[16,128]{1,0:T(8,128)} custom-call(f32[24,1024]{1,0:T(8,128)S(1)} %collective-permute-done.1.refs_0_, f32[24,1024]{1,0:T(8,128)S(1)} %collective-permute-done.refs_1_, f32[24,1024]{1,0:T(8,128)S(1)} %collective-permute-done.2.refs_2_, f32[24,1024]{1,0:T(8,128)S(1)} %collective-permute-done.3.refs_3_, ...), custom_call_target="tpu_custom_call" | custom-call | tf_op jit(solution)/shard_map/solve/pallas_call | solution.py:195
  (4 shorter events, 0.0 us)
Async XLA Ops:
  0.0 26.2 %copy-start = (s32[128]{0:T(128)S(1)}, s32[128]{0:T(128)}, u32[]{:S(2)}) copy-start(s32[128]{0:T(128)} %param.13) | copy-start | bytes 1540
  6.4 9.1 %collective-permute-start.8 = (f32[24,1024]{1,0:T(8,128)}, f32[24,1024]{1,0:T(8,128)S(1)}, u32[]{:S(2)}, u32[]{:S(2)}) collective-permute-start(f32[24,1024]{1,0:T(8,128)} %project.1), channel_id=1, source_target_pairs={{0,8},{1,9},{2,10},{3,11},{4,12},{5,13},{6,14},{7,15},{8,0},{9,1},... | collective-permute-start | bytes 294920 | tf_op jit(solution)/shard_map/ppermute | solution.py:207
  10.5 7.6 %collective-permute-start.6 = (f32[24,1024]{1,0:T(8,128)}, f32[24,1024]{1,0:T(8,128)S(1)}, u32[]{:S(2)}, u32[]{:S(2)}) collective-permute-start(f32[24,1024]{1,0:T(8,128)} %project.1), channel_id=1, source_target_pairs={{0,6},{1,7},{2,4},{3,5},{4,2},{5,3},{6,0},{7,1},{8,14},{9,15},{10,... | collective-permute-start | bytes 294920 | tf_op jit(solution)/shard_map/ppermute | solution.py:207
  13.0 6.6 %collective-permute-start.4 = (f32[24,1024]{1,0:T(8,128)}, f32[24,1024]{1,0:T(8,128)S(1)}, u32[]{:S(2)}, u32[]{:S(2)}) collective-permute-start(f32[24,1024]{1,0:T(8,128)} %project.1), channel_id=1, source_target_pairs={{0,4},{1,5},{2,6},{3,7},{4,0},{5,1},{6,2},{7,3},{8,12},{9,13},{10,... | collective-permute-start | bytes 294920 | tf_op jit(solution)/shard_map/ppermute | solution.py:207
  13.4 6.8 %collective-permute-start.2 = (f32[24,1024]{1,0:T(8,128)}, f32[24,1024]{1,0:T(8,128)S(1)}, u32[]{:S(2)}, u32[]{:S(2)}) collective-permute-start(f32[24,1024]{1,0:T(8,128)} %project.1), channel_id=1, source_target_pairs={{0,2},{1,3},{2,0},{3,1},{4,6},{5,7},{6,4},{7,5},{8,10},{9,11},{10,... | collective-permute-start | bytes 294920 | tf_op jit(solution)/shard_map/ppermute | solution.py:207
  14.0 6.3 %collective-permute-start = (f32[24,1024]{1,0:T(8,128)}, f32[24,1024]{1,0:T(8,128)S(1)}, u32[]{:S(2)}, u32[]{:S(2)}) collective-permute-start(f32[24,1024]{1,0:T(8,128)} %project.1), channel_id=1, source_target_pairs={{0,1},{1,0},{2,3},{3,2},{4,5},{5,4},{6,7},{7,6},{8,9},{9,8},{10,11... | collective-permute-start | bytes 294920 | tf_op jit(solution)/shard_map/ppermute | solution.py:207
  15.5 6.6 %collective-permute-start.14 = (f32[24,1024]{1,0:T(8,128)S(1)}, f32[24,1024]{1,0:T(8,128)S(1)}, u32[]{:S(2)}, u32[]{:S(2)}) collective-permute-start(f32[24,1024]{1,0:T(8,128)S(1)} %collective-permute-done.8.refs_8_), channel_id=1, source_target_pairs={{0,6},{1,7},{2,4},{3,5},{4,2},{5,3},{6,0},{7,1},{8,14},{9,15},{10,... | collective-permute-start | bytes 294920 | tf_op jit(solution)/shard_map/ppermute | solution.py:207
  18.0 5.0 %collective-permute-start.12 = (f32[24,1024]{1,0:T(8,128)S(1)}, f32[24,1024]{1,0:T(8,128)S(1)}, u32[]{:S(2)}, u32[]{:S(2)}) collective-permute-start(f32[24,1024]{1,0:T(8,128)S(1)} %collective-permute-done.8.refs_8_), channel_id=1, source_target_pairs={{0,4},{1,5},{2,6},{3,7},{4,0},{5,1},{6,2},{7,3},{8,12},{9,13},{10,... | collective-permute-start | bytes 294920 | tf_op jit(solution)/shard_map/ppermute | solution.py:207
  19.6 4.6 %collective-permute-start.10 = (f32[24,1024]{1,0:T(8,128)S(1)}, f32[24,1024]{1,0:T(8,128)S(1)}, u32[]{:S(2)}, u32[]{:S(2)}) collective-permute-start(f32[24,1024]{1,0:T(8,128)S(1)} %collective-permute-done.8.refs_8_), channel_id=1, source_target_pairs={{0,2},{1,3},{2,0},{3,1},{4,6},{5,7},{6,4},{7,5},{8,10},{9,11},{10,... | collective-permute-start | bytes 294920 | tf_op jit(solution)/shard_map/ppermute | solution.py:207
  20.2 4.0 %collective-permute-start.9 = (f32[24,1024]{1,0:T(8,128)S(1)}, f32[24,1024]{1,0:T(8,128)S(1)}, u32[]{:S(2)}, u32[]{:S(2)}) collective-permute-start(f32[24,1024]{1,0:T(8,128)S(1)} %collective-permute-done.8.refs_8_), channel_id=1, source_target_pairs={{0,1},{1,0},{2,3},{3,2},{4,5},{5,4},{6,7},{7,6},{8,9},{9,8},{10,11... | collective-permute-start | bytes 294920 | tf_op jit(solution)/shard_map/ppermute | solution.py:207
  20.2 4.5 %collective-permute-start.7 = (f32[24,1024]{1,0:T(8,128)S(1)}, f32[24,1024]{1,0:T(8,128)S(1)}, u32[]{:S(2)}, u32[]{:S(2)}) collective-permute-start(f32[24,1024]{1,0:T(8,128)S(1)} %collective-permute-done.6.refs_6_), channel_id=1, source_target_pairs={{0,1},{1,0},{2,3},{3,2},{4,5},{5,4},{6,7},{7,6},{8,9},{9,8},{10,11... | collective-permute-start | bytes 294920 | tf_op jit(solution)/shard_map/ppermute | solution.py:207
  22.1 2.7 %collective-permute-start.5 = (f32[24,1024]{1,0:T(8,128)S(1)}, f32[24,1024]{1,0:T(8,128)S(1)}, u32[]{:S(2)}, u32[]{:S(2)}) collective-permute-start(f32[24,1024]{1,0:T(8,128)S(1)} %collective-permute-done.4.refs_4_), channel_id=1, source_target_pairs={{0,1},{1,0},{2,3},{3,2},{4,5},{5,4},{6,7},{7,6},{8,9},{9,8},{10,11... | collective-permute-start | bytes 294920 | tf_op jit(solution)/shard_map/ppermute | solution.py:207
  23.1 2.2 %collective-permute-start.3 = (f32[24,1024]{1,0:T(8,128)S(1)}, f32[24,1024]{1,0:T(8,128)S(1)}, u32[]{:S(2)}, u32[]{:S(2)}) collective-permute-start(f32[24,1024]{1,0:T(8,128)S(1)} %collective-permute-done.2.refs_2_), channel_id=1, source_target_pairs={{0,1},{1,0},{2,3},{3,2},{4,5},{5,4},{6,7},{7,6},{8,9},{9,8},{10,11... | collective-permute-start | bytes 294920 | tf_op jit(solution)/shard_map/ppermute | solution.py:207
  24.2 1.3 %collective-permute-start.1 = (f32[24,1024]{1,0:T(8,128)S(1)}, f32[24,1024]{1,0:T(8,128)S(1)}, u32[]{:S(2)}, u32[]{:S(2)}) collective-permute-start(f32[24,1024]{1,0:T(8,128)S(1)} %collective-permute-done.refs_1_), channel_id=1, source_target_pairs={{0,1},{1,0},{2,3},{3,2},{4,5},{5,4},{6,7},{7,6},{8,9},{9,8},{10,11... | collective-permute-start | bytes 294920 | tf_op jit(solution)/shard_map/ppermute | solution.py:207
  24.2 1.5 %collective-permute-start.15 = (f32[24,1024]{1,0:T(8,128)S(1)}, f32[24,1024]{1,0:T(8,128)S(1)}, u32[]{:S(2)}, u32[]{:S(2)}) collective-permute-start(f32[24,1024]{1,0:T(8,128)S(1)} %collective-permute-done.14.refs_14_), channel_id=1, source_target_pairs={{0,1},{1,0},{2,3},{3,2},{4,5},{5,4},{6,7},{7,6},{8,9},{9,8},{10,11... | collective-permute-start | bytes 294920 | tf_op jit(solution)/shard_map/ppermute | solution.py:207
  24.7 1.3 %collective-permute-start.13 = (f32[24,1024]{1,0:T(8,128)S(1)}, f32[24,1024]{1,0:T(8,128)S(1)}, u32[]{:S(2)}, u32[]{:S(2)}) collective-permute-start(f32[24,1024]{1,0:T(8,128)S(1)} %collective-permute-done.12.refs_12_), channel_id=1, source_target_pairs={{0,1},{1,0},{2,3},{3,2},{4,5},{5,4},{6,7},{7,6},{8,9},{9,8},{10,11... | collective-permute-start | bytes 294920 | tf_op jit(solution)/shard_map/ppermute | solution.py:207
  24.8 1.4 %collective-permute-start.11 = (f32[24,1024]{1,0:T(8,128)S(1)}, f32[24,1024]{1,0:T(8,128)S(1)}, u32[]{:S(2)}, u32[]{:S(2)}) collective-permute-start(f32[24,1024]{1,0:T(8,128)S(1)} %collective-permute-done.10.refs_10_), channel_id=1, source_target_pairs={{0,1},{1,0},{2,3},{3,2},{4,5},{5,4},{6,7},{7,6},{8,9},{9,8},{10,11... | collective-permute-start | bytes 294920 | tf_op jit(solution)/shard_map/ppermute | solution.py:207
